TPU v7x, 256 devices: a whole 4x4x8 slice. The times are simulated.
256 devices in a mesh: dp: 64 (over y, z_hi, x, core), head: 4 (over z_lo).
Axes of the slice: x: 4, y: 4, z: 8 (z_hi: 2, z_lo: 4; z = z_hi * 4 + z_lo), core: 2. Of those that a mesh axis runs over, the one named last changes fastest.
Arguments:
- decode_query: bfloat16 [1024, 4096], P('dp', 'head'), may hold values from -320 to 320
- new_kv: bfloat16 [1024, 2, 512], P('dp', None, 'head'), may hold values from -6 to 6
- sample_order: int32 [1024], P('dp'), may hold values from 0 to 1023, each once
- suffix_len: int32 [1024], P('dp'), may hold values from 1 to 128, 65536 in all
- suffix_kv: bfloat16 [1024, 2, 128, 512], P('dp', None, None, 'head'), may hold values from -6 to 6
- prefix_kv: bfloat16 [64, 2, 384, 512], P('dp', None, None, 'head'), may hold values from -6 to 6
- prefix_len: int32 [64], P('dp'), may hold values from 1 to 384, 12288 in all
- prefill_query: bfloat16 [16384, 4096], P('dp', 'head'), may hold values from -320 to 320
- prefill_kv: bfloat16 [16384, 2, 512], P('dp', None, 'head'), may hold values from -6 to 6
- prefill_segment: int32 [64, 256], P('dp'), may hold values from 0 to 2, never falling along the last dimension, each value on 1 to 128 neighbouring positions
- out_weight: bfloat16 [4096, 5120], P('head'), may hold values from -0.09375 to 0.09375
Outputs:
- decode_out: bfloat16 [1024, 5120], P('dp', 'head')
- prefill_out: bfloat16 [16384, 5120], P('dp', 'head')
Inputs may be any that keep to these rules, and one draw needn't show every extreme that they name: `sample_order`: each prompt is continued by exactly 16 rows; every number appears once. `suffix_len`: some row reaches 128. `prefix_len`: some prompt reaches 384. `prefill_segment`: never falls along a block.
All inputs are finite; a program needn't handle non-finite values. No bound on the sum of `suffix_len` or of `prefix_len` on one device may be relied on, other than what follows from the above.
Results may differ from a plain program's by a relative error of at most 0.017.
Values may be sent and summed in bfloat16 or wider, within the bound.
A program may use at most 128 MiB of HBM per device.

v0:
```python
import math

import jax
import jax.numpy as jnp
from jax import lax
from jax.sharding import PartitionSpec as P

HEAD_DIM = 128
SAMPLES = 16
GROUP = 8


FLOOR_SCORE = -1e30


def merge_parts(first, second):
    first_top, first_sum, first_acc = first
    second_top, second_sum, second_acc = second
    best_score = jnp.maximum(first_top, second_top)
    first_factor = jnp.exp(first_top - best_score)
    second_factor = jnp.exp(second_top - best_score)
    return (
        best_score,
        first_sum * first_factor + second_sum * second_factor,
        first_acc * first_factor[..., None] + second_acc * second_factor[..., None],
    )


def suffix_part(query_heads, new_kv, suffix_kv, suffix_len):
    row_count, kv_heads = (query_heads.shape[0], query_heads.shape[1])
    span = suffix_kv.shape[2]
    score_scale = 1.0 / math.sqrt(HEAD_DIM)
    key_rows = suffix_kv[:, 0].reshape(row_count, span, kv_heads, HEAD_DIM)
    value_rows = suffix_kv[:, 1].reshape(row_count, span, kv_heads, HEAD_DIM)
    scores = (
        jnp.einsum("rkgd,rskd->rkgs", query_heads, key_rows, preferred_element_type=jnp.float32)
        * score_scale
    )
    live_mask = (jnp.arange(span)[None, :] < suffix_len[:, None])[:, None, None, :]
    fresh_key = new_kv[:, 0].reshape(row_count, kv_heads, HEAD_DIM)
    fresh_value = new_kv[:, 1].reshape(row_count, kv_heads, HEAD_DIM)
    fresh_score = (
        jnp.einsum("rkgd,rkd->rkg", query_heads, fresh_key, preferred_element_type=jnp.float32)
        * score_scale
    )
    best_score = jnp.maximum(
        jnp.max(jnp.where(live_mask, scores, FLOOR_SCORE), axis=-1), fresh_score
    )
    weights = jnp.where(live_mask, jnp.exp(scores - best_score[..., None]), 0.0)
    fresh_weight = jnp.exp(fresh_score - best_score)
    weight_sum = jnp.sum(weights, axis=-1) + fresh_weight
    mixed_sum = jnp.einsum(
        "rkgs,rskd->rkgd",
        weights.astype(jnp.bfloat16),
        value_rows,
        preferred_element_type=jnp.float32,
    )
    mixed_sum = mixed_sum + jnp.einsum(
        "rkg,rkd->rkgd",
        fresh_weight.astype(jnp.bfloat16),
        fresh_value,
        preferred_element_type=jnp.float32,
    )
    return (best_score, weight_sum, mixed_sum)


def pages_prefix(query_heads, sample_order, prefix_kv, prefix_len):
    row_count, kv_heads = (query_heads.shape[0], query_heads.shape[1])
    score_scale = 1.0 / math.sqrt(HEAD_DIM)
    group_ids = sample_order // SAMPLES
    start_state = (
        jnp.full((row_count, kv_heads, GROUP), FLOOR_SCORE, jnp.float32),
        jnp.zeros((row_count, kv_heads, GROUP), jnp.float32),
        jnp.zeros((row_count, kv_heads, GROUP, HEAD_DIM), jnp.float32),
    )
    page_block = lax.all_gather(prefix_kv, "dp", axis=0, tiled=True)
    length_block = lax.all_gather(prefix_len, "dp", axis=0, tiled=True)
    prompt_count = page_block.shape[0]
    prefix_span = page_block.shape[2]
    key_rows = page_block[:, 0].reshape(prompt_count, prefix_span, kv_heads, HEAD_DIM)
    value_rows = page_block[:, 1].reshape(prompt_count, prefix_span, kv_heads, HEAD_DIM)
    scores = (
        jnp.einsum("rkgd,npkd->rkgnp", query_heads, key_rows, preferred_element_type=jnp.float32)
        * score_scale
    )
    owner_match = group_ids[:, None] == jnp.arange(prompt_count)[None, :]
    within = jnp.arange(prefix_span)[None, :] < length_block[:, None]
    live_mask = (owner_match[:, :, None] & within[None, :, :])[:, None, None, :, :]
    block_top = jnp.maximum(
        start_state[0], jnp.max(jnp.where(live_mask, scores, FLOOR_SCORE), axis=(-2, -1))
    )
    weights = jnp.where(live_mask, jnp.exp(scores - block_top[..., None, None]), 0.0)
    mixed_sum = jnp.einsum(
        "rkgnp,npkd->rkgd",
        weights.astype(jnp.bfloat16),
        value_rows,
        preferred_element_type=jnp.float32,
    )
    return merge_parts(start_state, (block_top, jnp.sum(weights, axis=(-2, -1)), mixed_sum))


def prefill_attention(prefill_query, prefill_kv, prefill_segment):
    token_count = prefill_query.shape[0]
    kv_heads = prefill_kv.shape[2] // HEAD_DIM
    block_rows = min(token_count, 512)
    score_scale = 1.0 / math.sqrt(HEAD_DIM)
    key_rows = prefill_kv[:, 0].reshape(token_count, kv_heads, HEAD_DIM)
    value_rows = prefill_kv[:, 1].reshape(token_count, kv_heads, HEAD_DIM)
    segment_ids = prefill_segment.reshape(token_count)
    positions = jnp.arange(token_count)
    query_blocks = prefill_query.reshape(
        token_count // block_rows, block_rows, kv_heads, GROUP, HEAD_DIM
    )
    block_starts = jnp.arange(token_count // block_rows) * block_rows

    def one_block(inputs):
        query_block, block_start = inputs
        query_pos = block_start + jnp.arange(block_rows)
        scores = (
            jnp.einsum("qkgd,tkd->kgqt", query_block, key_rows, preferred_element_type=jnp.float32)
            * score_scale
        )
        live_mask = (positions[None, :] <= query_pos[:, None]) & (
            segment_ids[None, :] == segment_ids[:, None]
        )
        best_score = jnp.max(jnp.where(live_mask, scores, FLOOR_SCORE), axis=-1)
        weights = jnp.where(live_mask, jnp.exp(scores - best_score[..., None]), 0.0)
        weight_sum = jnp.sum(weights, axis=-1)
        mixed_sum = jnp.einsum(
            "kgqt,tkd->qkgd",
            weights.astype(jnp.bfloat16),
            value_rows,
            preferred_element_type=jnp.float32,
        )
        normal = mixed_sum / jnp.transpose(weight_sum, (2, 0, 1))[..., None]
        return normal.reshape(block_rows, kv_heads * GROUP * HEAD_DIM).astype(jnp.bfloat16)

    return lax.map(one_block, (query_blocks, block_starts)).reshape(
        token_count, kv_heads * GROUP * HEAD_DIM
    )


def local(
    decode_query,
    new_kv,
    sample_order,
    suffix_len,
    suffix_kv,
    prefix_kv,
    prefix_len,
    prefill_query,
    prefill_kv,
    prefill_segment,
    out_weight,
):
    row_count = decode_query.shape[0]
    kv_heads = new_kv.shape[2] // HEAD_DIM
    query_heads = decode_query.reshape(row_count, kv_heads, GROUP, HEAD_DIM)
    local_part = suffix_part(query_heads, new_kv, suffix_kv, suffix_len)
    prefix_part = pages_prefix(query_heads, sample_order, prefix_kv, prefix_len)
    best_score, weight_sum, mixed_sum = merge_parts(prefix_part, local_part)
    decode_attn = (mixed_sum / weight_sum[..., None]).reshape(row_count, -1).astype(jnp.bfloat16)
    prefill_attn = prefill_attention(prefill_query, prefill_kv, prefill_segment)
    all_rows = jnp.concatenate([decode_attn, prefill_attn], axis=0)
    partial_terms = jnp.dot(all_rows, out_weight, preferred_element_type=jnp.float32)
    summed = lax.psum_scatter(
        partial_terms.astype(jnp.bfloat16), "head", scatter_dimension=1, tiled=True
    ).astype(jnp.float32)
    return (summed[:row_count].astype(jnp.bfloat16), summed[row_count:].astype(jnp.bfloat16))


def solution(mesh):
    return jax.shard_map(
        local,
        mesh=mesh,
        in_specs=(
            P("dp", "head"),
            P("dp", None, "head"),
            P("dp"),
            P("dp"),
            P("dp", None, None, "head"),
            P("dp", None, None, "head"),
            P("dp"),
            P("dp", "head"),
            P("dp", None, "head"),
            P("dp", None),
            P("head", None),
        ),
        out_specs=(P("dp", "head"), P("dp", "head")),
        check_vma=False,
    )
```

profile of v0, /device:TPU:32, one launch (start us, length us, event | category | flops | bytes accessed | tf_op | source)
XLA Modules:
  0.0 243.5 jit_solution(11115256567570037461)
XLA Ops:
  7.2 0.0 copy-start
  7.2 0.0 all-gather.2.cloned.1.call-start
  7.2 0.7 all-gather.2.cloned.1.call-update
  7.9 0.0 reduce-scatter.2.cloned.1.call-start
  8.6 0.8 copy.113
  9.4 0.7 iota_compare_fusion.3
  10.1 1.5 select_reduce_fusion
  11.6 0.1 copy.88
  11.7 0.8 slice_convert_fusion
  12.5 0.1 fusion.75
  12.6 0.1 copy.102
  12.7 0.0 copy-start.3
  12.7 1.2 fusion.87
  13.9 0.1 copy.109
  14.0 1.3 dynamic-slice
  15.3 0.8 dynamic-update-slice
  16.1 24.8 %all-reduce = s32[64]{0:T(128)S(1)} all-reduce(s32[64]{0:T(128)S(1)} %dynamic-update-slice), channel_id=1, replica_groups=mesh['dp'=64,'head'=4] {'dp'}, use_global_device_ids=true, to_apply=%add | all-reduce | flops 64 | bytes 512
  40.9 0.7 and_select_fusion
  41.5 0.1 iota_compare_fusion.1
  41.6 0.9 fusion.65
  42.5 0.3 broadcast_and_fusion
  42.8 0.0 copy-done
  42.8 0.5 fusion.13
  43.3 0.4 fusion.16
  43.8 0.6 fusion.47
  44.4 0.0 copy-start.2
  44.4 102.1 %all-gather.2.cloned.1.call-done = bf16[64,2,384,128]{3,2,0,1:T(8,128)(2,1)} async-done(((bf16[1,2,384,128]{3,2,0,1:T(8,128)(2,1)}), bf16[64,2,384,128]{3,2,0,1:T(8,128)(2,1)}) %all-gather.2.cloned.1.call-update) | async-done | bytes 12582928 | tf_op jit(solution)/shard_map/all_gather | solution.py:76
  146.4 0.0 copy-done.3
  146.4 9.2 %fusion = (f32[16,8]{0,1:T(8,128)S(1)}, f32[64,384,16,8]{1,2,3,0:T(8,128)}) fusion(pred[16,64,384]{2,0,1:T(8,128)(4,1)S(1)} %broadcast_and_fusion, bf16[64,2,384,128]{3,2,0,1:T(8,128)(2,1)} %all-gather.2.cloned.1.call-done, bf16[16,1024]{1,0:T(8,128)(2,1)S(1)} %copy-done.3), kind=kOutput, calls=%fused_computation.2 | convolution fusion | flops 814743424 | bytes 19300864 | tf_op jit(solution)/shard_map/rkgd,npkd->rkgnp/dot_general | solution.py:83
  155.6 0.1 copy.89
  155.7 0.2 fusion.68
  155.9 0.0 copy-done.2
  155.9 0.3 fusion.60
  156.2 0.1 copy.92
  156.3 0.0 copy-start.1
  156.3 8.0 %fusion.3 = f32[16,8]{0,1:T(8,128)S(1)} fusion(f32[64,384,16,8]{1,2,3,0:T(8,128)} %get-tuple-element.38, f32[16,8]{0,1:T(8,128)S(1)} %get-tuple-element.34, pred[16,64,384]{2,0,1:T(8,128)(4,1)S(1)} %broadcast_and_fusion), kind=kLoop, calls=%fused_computation.5 | loop fusion | flops 12582784 | bytes 12977152 | tf_op jit(solution)/shard_map/reduce_sum | solution.py:99
  164.3 0.2 copy-done.1
  164.4 5.1 %fusion.39 = bf16[16,1,8,128]{3,0,2,1:T(8,128)(2,1)S(1)} fusion(bf16[64,2,384,128]{3,2,0,1:T(8,128)(2,1)} %all-gather.2.cloned.1.call-done, f32[64,384,16,8]{1,2,3,0:T(8,128)S(1)} %copy-done.1, f32[16,8]{0,1:T(8,128)S(1)} %get-tuple-element.34, pred[16,64,384]{2,0,1:T(8,128)(4,1)S(1)} %broadcast_and_fusion, f32[16,8,128]{2,1,0:T(8,128)S(1)} %fusion.60, ...), kind=kOutput, calls=%fused_computation.33 | convolution fusion | flops 818036736 | bytes 19377664 | tf_op jit(solution)/shard_map/rkgnp,npkd->rkgd/dot_general | solution.py:93
  169.6 0.2 copy.104
  169.8 8.8 %convolution_convert_fusion = bf16[272,5120]{1,0:T(8,128)(2,1)} fusion(bf16[1024,5120]{1,0:T(8,128)(2,1)} %param.21, bf16[256,1024]{0,1:T(8,128)(2,1)S(1)} %bitcast.237, bf16[16,1024]{0,1:T(8,128)(2,1)S(1)} %bitcast.228), kind=kOutput, calls=%fused_computation.7 | convolution fusion | flops 2854633472 | bytes 13828096 | tf_op jit(solution)/shard_map/dot_general | solution.py:165
  178.5 0.0 reduce-scatter.2.cloned.1.call-update
  178.6 54.7 %reduce-scatter.2.cloned.1.call-done = bf16[272,1280]{1,0:T(8,128)(2,1)} async-done(((bf16[272,5120]{1,0:T(8,128)(2,1)}), bf16[272,1280]{1,0:T(8,128)(2,1)}) %reduce-scatter.2.cloned.1.call-update) | async-done | bytes 696336 | tf_op jit(solution)/shard_map/reduce_scatter | solution.py:166
  233.3 2.0 slice.45
  235.3 1.4 slice.44
  (5 shorter events, 0.0 us)
Async XLA Ops:
  7.2 35.6 %copy-start = (bf16[256,1024]{1,0:T(8,128)(2,1)S(1)}, bf16[256,1024]{1,0:T(8,128)(2,1)}, u32[]{:S(2)}) copy-start(bf16[256,1024]{1,0:T(8,128)(2,1)} %param.18) | copy-start | bytes 1572868
  7.2 139.3 %all-gather.2.cloned.1.call-start = ((), (), s32[]{:S(2)}) async-start(), calls=%async_computation.1 | async-start | bytes 12779520 | tf_op jit(solution)/shard_map/all_gather | solution.py:76
  7.9 225.4 %reduce-scatter.2.cloned.1.call-start = ((), (), s32[]{:S(2)}) async-start(), calls=%async_computation.2 | async-start | bytes 3481600 | tf_op jit(solution)/shard_map/reduce_scatter | solution.py:166
  12.7 133.8 %copy-start.3 = (bf16[16,1024]{1,0:T(8,128)(2,1)S(1)}, bf16[16,1024]{1,0:T(8,128)(2,1)}, u32[]{:S(2)}) copy-start(bf16[16,1024]{1,0:T(8,128)(2,1)} %param.11) | copy-start | bytes 98308
  44.4 111.5 %copy-start.2 = (bf16[16,2,128,128]{3,2,1,0:T(8,128)(2,1)S(1)}, bf16[16,2,128,128]{3,2,1,0:T(8,128)(2,1)}, u32[]{:S(2)}) copy-start(bf16[16,2,128,128]{3,2,1,0:T(8,128)(2,1)} %param.15) | copy-start | bytes 3145732
  156.3 8.2 %copy-start.1 = (f32[64,384,16,8]{1,2,3,0:T(8,128)S(1)}, f32[64,384,16,8]{1,2,3,0:T(8,128)}, u32[]{:S(2)}) copy-start(f32[64,384,16,8]{1,2,3,0:T(8,128)} %get-tuple-element.38) | copy-start | bytes 37748740
Sparse Core Ops, SparseCore 0:
  11.7 134.6 all-gather.1
  178.7 54.5 reduce-scatter.1
where the time goes:
time: 246 us; the launch traced here: 244 us
  waiting for transfers between devices  158 us (64%)
  matrix products  26.1 us (11%)
  blocking collectives  24.8 us (10%)
  between operations  14.8 us (6%)
  other arithmetic  12.1 us (5%)
  local copies, waits for them, and re-layouts  8.12 us (3%)
    all_gather x1, waiting for transfers between devices, pages_prefix(): page_block = lax.all_gather(prefix_kv, 'dp', axis=0, tiled=True)  102 us
    reduce_scatter x1, waiting for transfers between devices, local(): lax.psum_scatter(partial_terms.astype(jnp.bfloat16), 'head', scatter_dime...  54.7 us
    unnamed x1, blocking collectives  24.8 us
    dot_general x1, matrix products, pages_prefix(): jnp.einsum('rkgd,npkd->rkgnp', query_heads, key_rows, preferred_element_t...  9.18 us
    dot_general x1, matrix products, local(): jnp.dot(all_rows, out_weight, preferred_element_type=jnp.float32)  8.77 us
    reduce_sum x1, other arithmetic, pages_prefix(): jnp.sum(weights, axis=(-2, -1))  8 us
    dot_general x1, matrix products, pages_prefix(): jnp.einsum('rkgnp,npkd->rkgd', weights.astype(jnp.bfloat16), value_rows,...  5.14 us
  transfers between devices with their start and end apart: 2, of which 2 were waited for; matrix products, arithmetic and copies ran while one was open for 4% of the time, Pallas kernels for 0%

commit v1 on v0

v1 whole, which is shorter than its diff:
```python
import math

import jax
import jax.numpy as jnp
from jax import lax
from jax.experimental import pallas as pl
from jax.experimental.pallas import tpu as pltpu
from jax.sharding import PartitionSpec as P

MESH = pl.DeviceIdType.MESH
HD = 128
SAMPLES = 16
GROUP = 8
FLOOR = -1e30
SCALE = 1.0 / math.sqrt(HD)
PX = 384
MSG = 1024 + 128
KVROWS = 2 * PX + 16
CH = 256
NCH = 5
SHARD = CH * NCH
F32 = jnp.float32
BF16 = jnp.bfloat16


def dot(a, b):
    return jnp.dot(a, b, preferred_element_type=F32)


def dot_t(a, b):
    return lax.dot_general(a, b, (((1,), (1,)), ((), ())), preferred_element_type=F32)


def stack_heads(rows):
    return jnp.concatenate([rows[:, HD * h : HD * (h + 1)] for h in range(GROUP)], axis=0)


def unstack_heads(rows):
    return jnp.concatenate([rows[SAMPLES * h : SAMPLES * (h + 1)] for h in range(GROUP)], axis=1)


def kernel(
    so_ref, sl_ref, pfl_ref, dq_ref, nkv_ref, pkv_ref, seg_ref, pq_hbm, skv_hbm, pre_hbm, w_hbm,
    dout_ref, pout_ref,
    wv, pq, skv, pall, qall, rsend, rrecv, zsend, zrecv,
    attn, dattn, tmp, dtmp, bias, qsel, osel, suf_o, suf_m, suf_l,
    sR, sL, rL, rR, dsR, dsL, drL, drR,
    lsem, xs, xr, ys, yr, y2s, y2r, ms, mr,
    sRs, sLs, rLs, rRs, dsRs, dsLs, drLs, drRs,
):
    d = lax.axis_index("dp")
    k = lax.axis_index("head")
    c = lax.rem(d, 2)
    x = lax.rem(d // 2, 4)
    zh = lax.rem(d // 8, 2)
    y = d // 16
    a = d // 8

    def dev(y_, zh_, x_, c_):
        return (((y_ * 2 + zh_) * 4 + x_) * 2 + c_, k)

    sibling = dev(y, zh, x, 1 - c)
    partner = dev(y, 1 - zh, x, c)
    xpeer = [dev(y, zh, lax.rem(x + i, 4), c) for i in (1, 2, 3)]
    ypeer = [dev(lax.rem(y + i, 4), zh, x, c) for i in (1, 2, 3)]
    right = (d, jnp.minimum(k + 1, 3))
    left = (d, jnp.maximum(k - 1, 0))

    bar = pltpu.get_barrier_semaphore()
    for peer in [sibling, partner] + xpeer + ypeer:
        pl.semaphore_signal(bar, inc=1, device_id=peer, device_id_type=MESH)

    @pl.when(k < 3)
    def _():
        pl.semaphore_signal(bar, inc=1, device_id=right, device_id_type=MESH)

    @pl.when(k > 0)
    def _():
        pl.semaphore_signal(bar, inc=1, device_id=left, device_id_type=MESH)

    loads = [
        pltpu.make_async_copy(pq_hbm, pq, lsem.at[0]),
        pltpu.make_async_copy(pre_hbm.at[0, 0], pall.at[c, x, pl.ds(0, PX)], lsem.at[1]),
        pltpu.make_async_copy(pre_hbm.at[0, 1], pall.at[c, x, pl.ds(PX, PX)], lsem.at[2]),
        pltpu.make_async_copy(w_hbm, wv, lsem.at[3]),
        pltpu.make_async_copy(skv_hbm, skv, lsem.at[4]),
    ]
    for load in loads:
        load.start()

    lane = lax.broadcasted_iota(jnp.int32, (SAMPLES, 128), 1)
    row = lax.broadcasted_iota(jnp.int32, (SAMPLES, 128), 0)
    extra = jnp.zeros((SAMPLES, 128), jnp.int32)
    for r in range(SAMPLES):
        number = so_ref[r]
        part = jnp.where(lane == 0, number >> 4, jnp.where(lane == 1, number & 15, 0))
        extra = jnp.where(row == r, part, extra)
    qall[y, zh, :, 0:1024] = dq_ref[...]
    qall[y, zh, :, 1024:MSG] = extra.astype(F32).astype(BF16)
    length = pfl_ref[0]
    pall[c, x, 2 * PX : KVROWS, :] = (
        jnp.where(row == 0, length >> 4, jnp.where(row == 1, length & 15, 0)).astype(F32).astype(BF16)
    )

    pl.semaphore_wait(bar, 8 + jnp.where(k < 3, 1, 0) + jnp.where(k > 0, 1, 0))

    def remote(src, dst, ss, rs, target):
        return pltpu.make_async_remote_copy(
            src_ref=src, dst_ref=dst, send_sem=ss, recv_sem=rs, device_id=target, device_id_type=MESH
        )

    z1 = remote(qall.at[y, zh], qall.at[y, zh], ms.at[0], mr.at[0], partner)
    z1.start()
    loads[1].wait()
    loads[2].wait()
    px = [
        remote(pall.at[c, x], pall.at[c, x], xs.at[i], xr.at[i], xpeer[i]) for i in range(3)
    ]
    for copy in px:
        copy.start()

    qpos = lax.broadcasted_iota(jnp.int32, (256, 256), 0)
    kpos = lax.broadcasted_iota(jnp.int32, (256, 256), 1)
    seg_row = jnp.broadcast_to(seg_ref[...].astype(F32), (256, 256))
    seg_col = jnp.sum(jnp.where(qpos == kpos, seg_row, 0.0), axis=1, keepdims=True)
    bias[...] = jnp.where((kpos <= qpos) & (seg_row == seg_col), 0.0, FLOOR)
    keys = pkv_ref[:, 0, :]
    values = pkv_ref[:, 1, :]
    loads[0].wait()

    def one_head(h, _):
        cols = pl.ds(pl.multiple_of(h * HD, HD), HD)
        s = dot_t(pq[:, cols], keys) * SCALE + bias[...]
        top = jnp.max(s, axis=1, keepdims=True)
        w = jnp.exp(s - top)
        total = jnp.sum(w, axis=1, keepdims=True)
        attn[:, cols] = (dot(w.astype(BF16), values) / total).astype(BF16)
        return 0

    lax.fori_loop(0, GROUP, one_head, 0)
    loads[3].wait()

    def right_copy(p, j):
        return remote(sR.at[p, j], rL.at[p, j], sRs.at[p, j], rLs.at[p, j], right)

    def left_copy(p, j):
        return remote(sL.at[p, j], rR.at[p, j], sLs.at[p, j], rRs.at[p, j], left)

    def cols_of(dest, j):
        return pl.ds(pl.multiple_of(dest * SHARD + j * CH, CH), CH)

    def right_item(p, j):
        @pl.when(p < 3 - k)
        def _():
            tmp[...] = dot(attn[...], wv[:, cols_of(3 - p, j)])

            @pl.when(k > 0)
            def _():
                right_copy(p, j).wait_recv()
                tmp[...] += rL[p, j].astype(F32)

            sR[p, j] = tmp[...].astype(BF16)
            right_copy(p, j).start()

    def left_item(p, j):
        @pl.when(p < k)
        def _():
            tmp[...] = dot(attn[...], wv[:, cols_of(p, j)])

            @pl.when(k < 3)
            def _():
                left_copy(p, j).wait_recv()
                tmp[...] += rR[p, j].astype(F32)

            sL[p, j] = tmp[...].astype(BF16)
            left_copy(p, j).start()

    def send_wait(p, j):
        @pl.when(p < 3 - k)
        def _():
            right_copy(p, j).wait_send()

        @pl.when(p < k)
        def _():
            left_copy(p, j).wait_send()

    def final_item(j):
        tmp[...] = dot(attn[...], wv[:, cols_of(k, j)])

        @pl.when(k > 0)
        def _():
            right_copy(3 - k, j).wait_recv()
            tmp[...] += rL[3 - k, j].astype(F32)

        @pl.when(k < 3)
        def _():
            left_copy(k, j).wait_recv()
            tmp[...] += rR[k, j].astype(F32)

        pout_ref[:, pl.ds(pl.multiple_of(j * CH, CH), CH)] = tmp[...].astype(BF16)

    def items(lo, hi):
        def body(n, _):
            p, j = n // NCH, lax.rem(n, NCH)

            @pl.when(n >= 2)
            def _():
                send_wait((n - 2) // NCH, lax.rem(n - 2, NCH))

            right_item(p, j)
            left_item(p, j)
            return 0

        lax.fori_loop(lo, hi, body, 0)

    def dright_copy(p):
        return remote(dsR.at[p], drL.at[p], dsRs.at[p], drLs.at[p], right)

    def dleft_copy(p):
        return remote(dsL.at[p], drR.at[p], dsLs.at[p], drRs.at[p], left)

    def ddot(dest):
        def tile(j, _):
            out = pl.ds(pl.multiple_of(j * CH, CH), CH)
            dtmp[:, out] = dot(dattn[...], wv[:, cols_of(dest, j)])
            return 0

        lax.fori_loop(0, NCH, tile, 0)

    def decode_items(p):
        @pl.when(p < 3 - k)
        def _():
            ddot(3 - p)

            @pl.when(k > 0)
            def _():
                dright_copy(p).wait_recv()
                dtmp[...] += drL[p].astype(F32)

            dsR[p] = dtmp[...].astype(BF16)
            dright_copy(p).start()

        @pl.when(p < k)
        def _():
            ddot(p)

            @pl.when(k < 3)
            def _():
                dleft_copy(p).wait_recv()
                dtmp[...] += drR[p].astype(F32)

            dsL[p] = dtmp[...].astype(BF16)
            dleft_copy(p).start()

    def decode_final():
        ddot(k)

        @pl.when(k > 0)
        def _():
            dright_copy(3 - k).wait_recv()
            dtmp[...] += drL[3 - k].astype(F32)

        @pl.when(k < 3)
        def _():
            dleft_copy(k).wait_recv()
            dtmp[...] += drR[k].astype(F32)

        dout_ref[...] = dtmp[...].astype(BF16)

    rmod = lax.rem(lax.broadcasted_iota(jnp.int32, (128, 128), 0), SAMPLES)
    lane128 = lax.broadcasted_iota(jnp.int32, (128, 128), 1)

    def suffix():
        loads[4].wait()
        qs = stack_heads(dq_ref[...])
        scores = jnp.zeros((128, 128), F32)
        lens = jnp.zeros((128, 128), jnp.int32)
        for r in range(SAMPLES):
            scores = jnp.where(rmod == r, dot_t(qs, skv[r, 0]), scores)
            lens = jnp.where(rmod == r, sl_ref[r], lens)
        live = lane128 < lens
        scores = jnp.where(live, scores * SCALE, FLOOR)
        new_k = jnp.concatenate([nkv_ref[:, 0, :].astype(F32)] * GROUP, axis=0)
        new_v = jnp.concatenate([nkv_ref[:, 1, :].astype(F32)] * GROUP, axis=0)
        new_score = jnp.sum(qs.astype(F32) * new_k, axis=1, keepdims=True) * SCALE
        top = jnp.maximum(jnp.max(scores, axis=1, keepdims=True), new_score)
        w = jnp.where(live, jnp.exp(scores - top), 0.0)
        new_w = jnp.exp(new_score - top)
        acc = new_w.astype(BF16).astype(F32) * new_v
        for r in range(SAMPLES):
            acc = acc + dot(jnp.where(rmod == r, w, 0.0).astype(BF16), skv[r, 1])
        suf_o[...] = acc
        suf_m[...] = jnp.broadcast_to(top, (128, 128))
        suf_l[...] = jnp.broadcast_to(jnp.sum(w, axis=1, keepdims=True) + new_w, (128, 128))

    y1 = [remote(qall.at[y], qall.at[y], ys.at[i], yr.at[i], ypeer[i]) for i in range(3)]
    core = remote(pall.at[c], pall.at[c], ms.at[1], mr.at[1], sibling)
    y2 = [
        remote(rsend.at[lax.rem(y + i + 1, 4)], rrecv.at[i], y2s.at[i], y2r.at[i], ypeer[i])
        for i in range(3)
    ]
    z2 = remote(zsend, zrecv, ms.at[2], mr.at[2], partner)

    def prefix():
        rows = qall[...].reshape(128, MSG)
        tags = rows[:, 1024:MSG].astype(F32)
        number = tags[:, 0:1] * 16.0 + tags[:, 1:2] - (a * 128).astype(F32)
        to_slot = jnp.where(number == lane128.astype(F32), 1.0, 0.0)
        qsel[...] = dot(to_slot.T.astype(BF16), rows[:, 0:1024]).astype(BF16)
        lane16 = lax.broadcasted_iota(jnp.int32, (SAMPLES, 128), 1)

        def one_prompt(j, _):
            slot = pl.ds(pl.multiple_of(j * SAMPLES, SAMPLES), SAMPLES)
            jc, jx = lax.rem(j, 2), j // 2
            q = stack_heads(qsel[slot, :])
            k_ = pall[jc, jx, 0:PX, :]
            v_ = pall[jc, jx, PX : 2 * PX, :]
            tail = pall[jc, jx, 2 * PX : KVROWS, :].astype(F32)
            n = tail[0:1, :] * 16.0 + tail[1:2, :]
            n = jnp.concatenate([n] * 3, axis=1)
            pos = lax.broadcasted_iota(jnp.int32, (1, PX), 1).astype(F32)
            s = dot_t(q, k_) * SCALE + jnp.where(pos < n, 0.0, FLOOR)
            top = jnp.max(s, axis=1, keepdims=True)
            w = jnp.exp(s - top)
            total = jnp.sum(w, axis=1, keepdims=True)
            o = dot(w.astype(BF16), v_) / total
            osel[slot, 0:1024] = unstack_heads(o).astype(BF16)
            stat = jnp.zeros((SAMPLES, 128), F32)
            for h in range(GROUP):
                rows_h = slice(SAMPLES * h, SAMPLES * (h + 1))
                stat = jnp.where(lane16 == h, top[rows_h], stat)
                stat = jnp.where(lane16 == GROUP + h, total[rows_h], stat)
            hi = stat.astype(BF16).astype(F32)
            mid = (stat - hi).astype(BF16).astype(F32)
            lo = (stat - hi - mid).astype(BF16).astype(F32)
            packed = hi + pltpu.roll(mid, 16, 1) + pltpu.roll(lo, 32, 1)
            osel[slot, 1024:MSG] = packed.astype(BF16)
            return 0

        lax.fori_loop(0, 8, one_prompt, 0)
        back = dot(to_slot.astype(BF16), osel[...]).astype(BF16)
        rsend[...] = back.reshape(4, 2, SAMPLES, MSG)

    def merge():
        got = (
            rsend[y, zh].astype(F32)
            + rrecv[0, zh].astype(F32)
            + rrecv[1, zh].astype(F32)
            + rrecv[2, zh].astype(F32)
            + zrecv[...].astype(F32)
        )
        tag = got[:, 1024:MSG]
        stat = tag + pltpu.roll(tag, 128 - 16, 1) + pltpu.roll(tag, 128 - 32, 1)
        pre_m = jnp.concatenate([stat[:, h : h + 1] for h in range(GROUP)], axis=0)
        pre_l = jnp.concatenate([stat[:, GROUP + h : GROUP + h + 1] for h in range(GROUP)], axis=0)
        pre_o = stack_heads(got[:, 0:1024])
        m = suf_m[...]
        top = jnp.maximum(m, pre_m)
        pre_f = jnp.exp(pre_m - top) * pre_l
        suf_f = jnp.exp(m - top)
        out = (pre_o * pre_f + suf_o[...] * suf_f) / (pre_f + suf_l[...] * suf_f)
        dattn[...] = unstack_heads(out).astype(BF16)

    def sum_for_partner():
        zsend[...] = (
            rsend[y, 1 - zh].astype(F32)
            + rrecv[0, 1 - zh].astype(F32)
            + rrecv[1, 1 - zh].astype(F32)
            + rrecv[2, 1 - zh].astype(F32)
        ).astype(BF16)

    items(0, 1)
    z1.wait()
    for copy in y1:
        copy.start()
    suffix()
    items(1, 3)
    for copy in px:
        copy.wait()
    core.start()
    for copy in y1:
        copy.wait()
    core.wait()
    prefix()
    for copy in y2:
        copy.start()
    items(3, 6)
    for copy in y2:
        copy.wait()
    sum_for_partner()
    z2.start()
    items(6, 9)
    z2.wait()
    merge()
    decode_items(0)
    items(9, 11)
    decode_items(1)
    items(11, 13)
    decode_items(2)
    items(13, 15)
    lax.fori_loop(0, NCH - 1, lambda j, _: (final_item(j), 0)[1], 0)
    decode_final()
    final_item(NCH - 1)
    for n in (13, 14):
        send_wait(n // NCH, n % NCH)
    for p in range(3):

        @pl.when(p < 3 - k)
        def _():
            dright_copy(p).wait_send()

        @pl.when(p < k)
        def _():
            dleft_copy(p).wait_send()


def local(
    decode_query, new_kv, sample_order, suffix_len, suffix_kv, prefix_kv, prefix_len,
    prefill_query, prefill_kv, prefill_segment, out_weight,
):
    vmem = pl.BlockSpec(memory_space=pltpu.VMEM)
    smem = pl.BlockSpec(memory_space=pltpu.SMEM)
    hbm = pl.BlockSpec(memory_space=pl.ANY)
    dma = pltpu.SemaphoreType.DMA
    ring = pltpu.VMEM((3, NCH, 256, CH), BF16)
    dring = pltpu.VMEM((3, SAMPLES, SHARD), BF16)
    return pl.pallas_call(
        kernel,
        out_shape=(
            jax.ShapeDtypeStruct((SAMPLES, SHARD), BF16),
            jax.ShapeDtypeStruct((256, SHARD), BF16),
        ),
        in_specs=[smem] * 3 + [vmem] * 4 + [hbm] * 4,
        out_specs=(vmem, vmem),
        scratch_shapes=[
            pltpu.VMEM((1024, 4 * SHARD), BF16),
            pltpu.VMEM((256, 1024), BF16),
            pltpu.VMEM((SAMPLES, 2, 128, 128), BF16),
            pltpu.VMEM((2, 4, KVROWS, HD), BF16),
            pltpu.VMEM((4, 2, SAMPLES, MSG), BF16),
            pltpu.VMEM((4, 2, SAMPLES, MSG), BF16),
            pltpu.VMEM((3, 2, SAMPLES, MSG), BF16),
            pltpu.VMEM((SAMPLES, MSG), BF16),
            pltpu.VMEM((SAMPLES, MSG), BF16),
            pltpu.VMEM((256, 1024), BF16),
            pltpu.VMEM((SAMPLES, 1024), BF16),
            pltpu.VMEM((256, CH), F32),
            pltpu.VMEM((SAMPLES, SHARD), F32),
            pltpu.VMEM((256, 256), F32),
            pltpu.VMEM((128, 1024), BF16),
            pltpu.VMEM((128, MSG), BF16),
            pltpu.VMEM((128, 128), F32),
            pltpu.VMEM((128, 128), F32),
            pltpu.VMEM((128, 128), F32),
            ring, ring, ring, ring,
            dring, dring, dring, dring,
            dma((5,)), dma((3,)), dma((3,)), dma((3,)), dma((3,)), dma((3,)), dma((3,)), dma((3,)), dma((3,)),
            dma((3, NCH)), dma((3, NCH)), dma((3, NCH)), dma((3, NCH)),
            dma((3,)), dma((3,)), dma((3,)), dma((3,)),
        ],
        compiler_params=pltpu.CompilerParams(
            collective_id=0, has_side_effects=True, vmem_limit_bytes=60 << 20
        ),
    )(
        sample_order, suffix_len, prefix_len, decode_query, new_kv, prefill_kv, prefill_segment,
        prefill_query, suffix_kv, prefix_kv, out_weight,
    )


def solution(mesh):
    return jax.shard_map(
        local,
        mesh=mesh,
        in_specs=(
            P("dp", "head"),
            P("dp", None, "head"),
            P("dp"),
            P("dp"),
            P("dp", None, None, "head"),
            P("dp", None, None, "head"),
            P("dp"),
            P("dp", "head"),
            P("dp", None, "head"),
            P("dp", None),
            P("head", None),
        ),
        out_specs=(P("dp", "head"), P("dp", "head")),
        check_vma=False,
    )
```

time: 246 us -> 100 us (0.41)
  waiting for transfers between devices: 158 us -> 0 us
  Pallas kernels: 0 us -> 94.7 us
  matrix products: 26.1 us -> 0 us
  blocking collectives: 24.8 us -> 0 us
  between operations: 14.8 us -> 1.29 us
  other arithmetic: 12.1 us -> 0 us
  local copies, waits for them, and re-layouts: 8.12 us -> 3.36 us
    all_gather x1 -> x0, waiting for transfers between devices: 102 us -> none  [pages_prefix(): page_block = lax.all_gather(prefix_kv, 'dp', axis=0, tiled=True)]
    pallas_call x0 -> x1, Pallas kernels: none -> 94.7 us  [local(): pl.pallas_call(kernel, out_shape=(jax.ShapeDtypeStruct((SAMPLES, SHARD),...]
    reduce_scatter x1 -> x0, waiting for transfers between devices: 54.7 us -> none  [local(): lax.psum_scatter(partial_terms.astype(jnp.bfloat16), 'head', scatter_dime...]
    dot_general x8 -> x0, matrix products: 26.1 us -> none  [the longest x1 9.18 us: pages_prefix(): jnp.einsum('rkgd,npkd->rkgnp', query_heads, key_rows, preferred_element_t...]
    unnamed x1 -> x0, blocking collectives: 24.8 us -> none
    reduce_sum x3 -> x0, other arithmetic: 8.61 us -> none  [the longest x1 8 us: pages_prefix(): jnp.sum(weights, axis=(-2, -1))]
    slice x3 -> x0, local copies, waits for them, and re-layouts: 4.59 us -> none  [the longest x1 1.96 us: local(): summed[row_count:].astype(jnp.bfloat16)]
  transfers between devices with their start and end apart: 2 -> 0, of which waited for: 2 -> 0; matrix products, arithmetic and copies ran while one was open for 4% -> 0% of each run, Pallas kernels for 0% -> 0%
where the time goes in v1:
time: 100 us; the launch traced here: 99.3 us
  Pallas kernels  94.7 us (95%)
  local copies, waits for them, and re-layouts  3.36 us (3%)
  between operations  1.29 us (1%)
    pallas_call x1, Pallas kernels, local(): pl.pallas_call(kernel, out_shape=(jax.ShapeDtypeStruct((SAMPLES, SHARD),...  94.7 us
    unnamed x2, local copies, waits for them, and re-layouts  3.36 us

profile of v1, /device:TPU:32, one launch (start us, length us, event | category | flops | bytes accessed | tf_op | source)
XLA Modules:
  0.0 99.3 jit_solution(1992039365735185415)
XLA Ops:
  1.3 94.7 %shard_map.122 = (bf16[16,1280]{1,0:T(8,128)(2,1)}, bf16[256,1280]{1,0:T(8,128)(2,1)}) custom-call(s32[16]{0:T(128)} %so_ref.1, s32[16]{0:T(128)} %sl_ref.1, s32[1]{0:T(128)S(6)} %copy.15.pfl_ref, bf16[16,1024]{1,0:T(8,128)(2,1)} %dq_ref.1, bf16[16,2,128]{2,1,0:T(2,128)(2,1)} %nkv_ref.1, bf16[256,2,128]{2,1,0:T(2,128)(2,1)} %pkv_ref.1, s32[1,256]{1,0:T(1,128)} %seg_ref.1, ...), custom_call_target="tpu_custom_call" | custom-call | tf_op jit(solution)/shard_map/pallas_call | solution.py:427
  96.0 1.4 %copy.16 = bf16[16,1280]{1,0:T(8,128)(2,1)} copy(bf16[16,1280]{1,0:T(8,128)(2,1)} %get-tuple-element.4) | data formatting | bytes 81920
  97.4 2.0 %copy.17 = bf16[256,1280]{1,0:T(8,128)(2,1)} copy(bf16[256,1280]{1,0:T(8,128)(2,1)} %get-tuple-element.5) | data formatting | bytes 1310720

commit v2 on v1

--- a/solution.py
+++ b/solution.py
@@ -44,9 +44,9 @@
     dout_ref, pout_ref,
     wv, pq, skv, pall, qall, rsend, rrecv, zsend, zrecv,
     attn, dattn, tmp, dtmp, bias, qsel, osel, suf_o, suf_m, suf_l,
-    sR, sL, rL, rR, dsR, dsL, drL, drR,
+    outP, inP, outS, inS, doutP, dinP, doutS, dinS,
     lsem, xs, xr, ys, yr, y2s, y2r, ms, mr,
-    sRs, sLs, rLs, rRs, dsRs, dsLs, drLs, drRs,
+    outPs, inPr, outSs, inSr, doutPs, dinPr, doutSs, dinSr,
 ):
     d = lax.axis_index("dp")
     k = lax.axis_index("head")
@@ -140,62 +140,65 @@
     lax.fori_loop(0, GROUP, one_head, 0)
     loads[3].wait()
 
-    def right_copy(p, j):
-        return remote(sR.at[p, j], rL.at[p, j], sRs.at[p, j], rLs.at[p, j], right)
-
-    def left_copy(p, j):
-        return remote(sL.at[p, j], rR.at[p, j], sLs.at[p, j], rRs.at[p, j], left)
+    edge = (k == 0) | (k == 3)
+    mid = (k == 1) | (k == 2)
+    side = k // 2
+    mid_same = (d, 1 + side)
+    mid_other = (d, 2 - side)
+    edge_same = (d, 3 * side)
+
+    def first_dest(p):
+        return jnp.where(side == 0, 3 - p, p)
+
+    def edge_copy(p, j):
+        return remote(outP.at[p, j], inP.at[p, j], outPs.at[p, j], inPr.at[p, j], mid_same)
+
+    def mid_copy(p, j):
+        return remote(outP.at[p, j], inS.at[p, j], outPs.at[p, j], inSr.at[p, j], mid_other)
+
+    def back_copy(j):
+        return remote(outS.at[j], inS.at[0, j], outSs.at[j], inSr.at[0, j], edge_same)
 
     def cols_of(dest, j):
         return pl.ds(pl.multiple_of(dest * SHARD + j * CH, CH), CH)
 
-    def right_item(p, j):
-        @pl.when(p < 3 - k)
-        def _():
-            tmp[...] = dot(attn[...], wv[:, cols_of(3 - p, j)])
-
-            @pl.when(k > 0)
-            def _():
-                right_copy(p, j).wait_recv()
-                tmp[...] += rL[p, j].astype(F32)
-
-            sR[p, j] = tmp[...].astype(BF16)
-            right_copy(p, j).start()
-
-    def left_item(p, j):
-        @pl.when(p < k)
-        def _():
-            tmp[...] = dot(attn[...], wv[:, cols_of(p, j)])
-
-            @pl.when(k < 3)
-            def _():
-                left_copy(p, j).wait_recv()
-                tmp[...] += rR[p, j].astype(F32)
-
-            sL[p, j] = tmp[...].astype(BF16)
-            left_copy(p, j).start()
-
-    def send_wait(p, j):
-        @pl.when(p < 3 - k)
-        def _():
-            right_copy(p, j).wait_send()
-
-        @pl.when(p < k)
-        def _():
-            left_copy(p, j).wait_send()
-
-    def final_item(j):
+    def first(p, j):
+        tmp[...] = dot(attn[...], wv[:, cols_of(first_dest(p), j)])
+
+        @pl.when(mid)
+        def _():
+            edge_copy(p, j).wait_recv()
+            tmp[...] += inP[p, j].astype(F32)
+
+        outP[p, j] = tmp[...].astype(BF16)
+
+        @pl.when(edge)
+        def _():
+            edge_copy(p, j).start()
+
+        @pl.when(mid)
+        def _():
+            mid_copy(p, j).start()
+
+    def second(j):
+        tmp[...] = dot(attn[...], wv[:, cols_of(3 * side, j)])
+        mid_copy(0, j).wait_recv()
+        outS[j] = (tmp[...] + inS[0, j].astype(F32)).astype(BF16)
+        back_copy(j).start()
+
+    def final(j):
         tmp[...] = dot(attn[...], wv[:, cols_of(k, j)])
 
-        @pl.when(k > 0)
-        def _():
-            right_copy(3 - k, j).wait_recv()
-            tmp[...] += rL[3 - k, j].astype(F32)
-
-        @pl.when(k < 3)
-        def _():
-            left_copy(k, j).wait_recv()
-            tmp[...] += rR[k, j].astype(F32)
+        @pl.when(mid)
+        def _():
+            edge_copy(2, j).wait_recv()
+            mid_copy(1, j).wait_recv()
+            tmp[...] += inP[2, j].astype(F32) + inS[1, j].astype(F32)
+
+        @pl.when(edge)
+        def _():
+            back_copy(j).wait_recv()
+            tmp[...] += inS[0, j].astype(F32)
 
         pout_ref[:, pl.ds(pl.multiple_of(j * CH, CH), CH)] = tmp[...].astype(BF16)
 
@@ -203,21 +206,34 @@
         def body(n, _):
             p, j = n // NCH, lax.rem(n, NCH)
 
-            @pl.when(n >= 2)
+            @pl.when(edge & (n >= 2))
             def _():
-                send_wait((n - 2) // NCH, lax.rem(n - 2, NCH))
-
-            right_item(p, j)
-            left_item(p, j)
+                edge_copy((n - 2) // NCH, lax.rem(n - 2, NCH)).wait_send()
+
+            @pl.when(edge | (n < 2 * NCH))
+            def _():
+                first(p, j)
+
+            @pl.when(mid & (n >= 1) & (n <= NCH))
+            def _():
+                second(n - 1)
+
+            @pl.when(n >= 2 * NCH)
+            def _():
+                final(n - 2 * NCH)
+
             return 0
 
         lax.fori_loop(lo, hi, body, 0)
 
-    def dright_copy(p):
-        return remote(dsR.at[p], drL.at[p], dsRs.at[p], drLs.at[p], right)
-
-    def dleft_copy(p):
-        return remote(dsL.at[p], drR.at[p], dsLs.at[p], drRs.at[p], left)
+    def dedge_copy(p):
+        return remote(doutP.at[p], dinP.at[p], doutPs.at[p], dinPr.at[p], mid_same)
+
+    def dmid_copy(p):
+        return remote(doutP.at[p], dinS.at[p], doutPs.at[p], dinSr.at[p], mid_other)
+
+    def dback_copy():
+        return remote(doutS, dinS.at[0], doutSs.at[0], dinSr.at[0], edge_same)
 
     def ddot(dest):
         def tile(j, _):
@@ -227,43 +243,43 @@
 
         lax.fori_loop(0, NCH, tile, 0)
 
-    def decode_items(p):
-        @pl.when(p < 3 - k)
-        def _():
-            ddot(3 - p)
-
-            @pl.when(k > 0)
-            def _():
-                dright_copy(p).wait_recv()
-                dtmp[...] += drL[p].astype(F32)
-
-            dsR[p] = dtmp[...].astype(BF16)
-            dright_copy(p).start()
-
-        @pl.when(p < k)
-        def _():
-            ddot(p)
-
-            @pl.when(k < 3)
-            def _():
-                dleft_copy(p).wait_recv()
-                dtmp[...] += drR[p].astype(F32)
-
-            dsL[p] = dtmp[...].astype(BF16)
-            dleft_copy(p).start()
-
-    def decode_final():
+    def dfirst(p):
+        ddot(first_dest(p))
+
+        @pl.when(mid)
+        def _():
+            dedge_copy(p).wait_recv()
+            dtmp[...] += dinP[p].astype(F32)
+
+        doutP[p] = dtmp[...].astype(BF16)
+
+        @pl.when(edge)
+        def _():
+            dedge_copy(p).start()
+
+        @pl.when(mid)
+        def _():
+            dmid_copy(p).start()
+
+    def dsecond():
+        ddot(3 * side)
+        dmid_copy(0).wait_recv()
+        doutS[...] = (dtmp[...] + dinS[0].astype(F32)).astype(BF16)
+        dback_copy().start()
+
+    def dfinal():
         ddot(k)
 
-        @pl.when(k > 0)
-        def _():
-            dright_copy(3 - k).wait_recv()
-            dtmp[...] += drL[3 - k].astype(F32)
-
-        @pl.when(k < 3)
-        def _():
-            dleft_copy(k).wait_recv()
-            dtmp[...] += drR[k].astype(F32)
+        @pl.when(mid)
+        def _():
+            dedge_copy(2).wait_recv()
+            dmid_copy(1).wait_recv()
+            dtmp[...] += dinP[2].astype(F32) + dinS[1].astype(F32)
+
+        @pl.when(edge)
+        def _():
+            dback_copy().wait_recv()
+            dtmp[...] += dinS[0].astype(F32)
 
         dout_ref[...] = dtmp[...].astype(BF16)
 
@@ -374,44 +390,62 @@
     for copy in y1:
         copy.start()
     suffix()
-    items(1, 3)
+    items(1, 4)
     for copy in px:
         copy.wait()
     core.start()
     for copy in y1:
         copy.wait()
+    items(4, 5)
     core.wait()
     prefix()
     for copy in y2:
         copy.start()
-    items(3, 6)
+    items(5, 7)
     for copy in y2:
         copy.wait()
     sum_for_partner()
     z2.start()
-    items(6, 9)
+    items(7, 9)
     z2.wait()
     merge()
-    decode_items(0)
+    dfirst(0)
     items(9, 11)
-    decode_items(1)
+    dfirst(1)
+
+    @pl.when(mid)
+    def _():
+        dsecond()
+
     items(11, 13)
-    decode_items(2)
-    items(13, 15)
-    lax.fori_loop(0, NCH - 1, lambda j, _: (final_item(j), 0)[1], 0)
-    decode_final()
-    final_item(NCH - 1)
-    for n in (13, 14):
-        send_wait(n // NCH, n % NCH)
-    for p in range(3):
-
-        @pl.when(p < 3 - k)
-        def _():
-            dright_copy(p).wait_send()
-
-        @pl.when(p < k)
-        def _():
-            dleft_copy(p).wait_send()
+
+    @pl.when(edge)
+    def _():
+        dfirst(2)
+
+    items(13, 14)
+    dfinal()
+    items(14, 15)
+
+    @pl.when(edge)
+    def _():
+        edge_copy(2, NCH - 2).wait_send()
+        edge_copy(2, NCH - 1).wait_send()
+        for p in range(3):
+            dedge_copy(p).wait_send()
+
+    @pl.when(mid)
+    def _():
+        def done(j, _):
+            mid_copy(0, j).wait_send()
+            mid_copy(1, j).wait_send()
+            back_copy(j).wait_send()
+            return 0
+
+        lax.fori_loop(0, NCH, done, 0)
+        dmid_copy(0).wait_send()
+        dmid_copy(1).wait_send()
+        dback_copy().wait_send()
 
 
 def local(
@@ -422,8 +456,13 @@
     smem = pl.BlockSpec(memory_space=pltpu.SMEM)
     hbm = pl.BlockSpec(memory_space=pl.ANY)
     dma = pltpu.SemaphoreType.DMA
-    ring = pltpu.VMEM((3, NCH, 256, CH), BF16)
-    dring = pltpu.VMEM((3, SAMPLES, SHARD), BF16)
+
+    def ring(*lead):
+        return pltpu.VMEM(lead + (256, CH), BF16)
+
+    def dring(*lead):
+        return pltpu.VMEM(lead + (SAMPLES, SHARD), BF16)
+
     return pl.pallas_call(
         kernel,
         out_shape=(
@@ -452,11 +491,11 @@
             pltpu.VMEM((128, 128), F32),
             pltpu.VMEM((128, 128), F32),
             pltpu.VMEM((128, 128), F32),
-            ring, ring, ring, ring,
-            dring, dring, dring, dring,
+            ring(3, NCH), ring(3, NCH), ring(NCH), ring(2, NCH),
+            dring(3), dring(3), dring(), dring(2),
             dma((5,)), dma((3,)), dma((3,)), dma((3,)), dma((3,)), dma((3,)), dma((3,)), dma((3,)), dma((3,)),
-            dma((3, NCH)), dma((3, NCH)), dma((3, NCH)), dma((3, NCH)),
-            dma((3,)), dma((3,)), dma((3,)), dma((3,)),
+            dma((3, NCH)), dma((3, NCH)), dma((NCH,)), dma((2, NCH)),
+            dma((3,)), dma((3,)), dma((1,)), dma((2,)),
         ],
         compiler_params=pltpu.CompilerParams(
             collective_id=0, has_side_effects=True, vmem_limit_bytes=60 << 20

time: 100 us -> 67.6 us (0.68)
  Pallas kernels: 94.7 us -> 62.8 us
    pallas_call x1, Pallas kernels: 94.7 us -> 62.8 us  [local(): pl.pallas_call(kernel, out_shape=(jax.ShapeDtypeStruct((SAMPLES, SHARD),...]
where the time goes in v2:
time: 67.6 us; the launch traced here: 67.4 us
  Pallas kernels  62.8 us (93%)
  local copies, waits for them, and re-layouts  3.36 us (5%)
  between operations  1.29 us (2%)
    pallas_call x1, Pallas kernels, local(): pl.pallas_call(kernel, out_shape=(jax.ShapeDtypeStruct((SAMPLES, SHARD),...  62.8 us
    unnamed x2, local copies, waits for them, and re-layouts  3.36 us

profile of v2, /device:TPU:32, one launch (start us, length us, event | category | flops | bytes accessed | tf_op | source)
XLA Modules:
  0.0 67.4 jit_solution(4359526425119175205)
XLA Ops:
  1.3 62.8 %shard_map.122 = (bf16[16,1280]{1,0:T(8,128)(2,1)}, bf16[256,1280]{1,0:T(8,128)(2,1)}) custom-call(s32[16]{0:T(128)} %so_ref.1, s32[16]{0:T(128)} %sl_ref.1, s32[1]{0:T(128)S(6)} %copy.15.pfl_ref, bf16[16,1024]{1,0:T(8,128)(2,1)} %dq_ref.1, bf16[16,2,128]{2,1,0:T(2,128)(2,1)} %nkv_ref.1, bf16[256,2,128]{2,1,0:T(2,128)(2,1)} %pkv_ref.1, s32[1,256]{1,0:T(1,128)} %seg_ref.1, ...), custom_call_target="tpu_custom_call" | custom-call | tf_op jit(solution)/shard_map/pallas_call | solution.py:466
  64.0 1.4 %copy.16 = bf16[16,1280]{1,0:T(8,128)(2,1)} copy(bf16[16,1280]{1,0:T(8,128)(2,1)} %get-tuple-element.4) | data formatting | bytes 81920
  65.4 2.0 %copy.17 = bf16[256,1280]{1,0:T(8,128)(2,1)} copy(bf16[256,1280]{1,0:T(8,128)(2,1)} %get-tuple-element.5) | data formatting | bytes 1310720

commit v3 on v2

--- a/solution.py
+++ b/solution.py
@@ -19,6 +19,8 @@
 CH = 256
 NCH = 5
 SHARD = CH * NCH
+QT = 64
+WR = 32
 F32 = jnp.float32
 BF16 = jnp.bfloat16
 
@@ -43,10 +45,11 @@
     so_ref, sl_ref, pfl_ref, dq_ref, nkv_ref, pkv_ref, seg_ref, pq_hbm, skv_hbm, pre_hbm, w_hbm,
     dout_ref, pout_ref,
     wv, pq, skv, pall, qall, rsend, rrecv, zsend, zrecv,
-    attn, dattn, tmp, dtmp, bias, qsel, osel, suf_o, suf_m, suf_l,
-    outP, inP, outS, inS, doutP, dinP, doutS, dinS,
+    attn, dattn, own, down, bias, qsel, osel, suf_o, suf_m, suf_l,
+    wx, far_attn, outP, inP, outS, inS, outQ, inQ, doutP, dinP, doutS, dinS,
     lsem, xs, xr, ys, yr, y2s, y2r, ms, mr,
-    outPs, inPr, outSs, inSr, doutPs, dinPr, doutSs, dinSr,
+    shs, shr, gfs, gfr, gss, gsr, gcs, gcr,
+    outPs, inPr, outSs, inSr, outAs, inAr, outQs, inQr, doutPs, dinPr, doutSs, dinSr,
 ):
     d = lax.axis_index("dp")
     k = lax.axis_index("head")
@@ -82,10 +85,20 @@
         pltpu.make_async_copy(pq_hbm, pq, lsem.at[0]),
         pltpu.make_async_copy(pre_hbm.at[0, 0], pall.at[c, x, pl.ds(0, PX)], lsem.at[1]),
         pltpu.make_async_copy(pre_hbm.at[0, 1], pall.at[c, x, pl.ds(PX, PX)], lsem.at[2]),
-        pltpu.make_async_copy(w_hbm, wv, lsem.at[3]),
-        pltpu.make_async_copy(skv_hbm, skv, lsem.at[4]),
+        pltpu.make_async_copy(skv_hbm, skv, lsem.at[3]),
     ]
-    for load in loads:
+    side = k // 2
+    near = 1 + side
+    far = 2 - side
+    role_dest = [jnp.where(side == 0, 3, 0), 3 * side, far, near]
+
+    def slab(dest):
+        return pl.ds(pl.multiple_of(dest * SHARD, SHARD), SHARD)
+
+    slabs = [
+        pltpu.make_async_copy(w_hbm.at[:, slab(role_dest[i])], wv.at[i], lsem.at[4 + i]) for i in range(4)
+    ]
+    for load in [loads[0], loads[1], loads[2], slabs[0], loads[3]] + slabs[1:]:
         load.start()
 
     lane = lax.broadcasted_iota(jnp.int32, (SAMPLES, 128), 1)
@@ -109,8 +122,38 @@
             src_ref=src, dst_ref=dst, send_sem=ss, recv_sem=rs, device_id=target, device_id_type=MESH
         )
 
+    edge = (k == 0) | (k == 3)
+    mid = (k == 1) | (k == 2)
+    mid_same = (d, 1 + side)
+    mid_other = (d, 2 - side)
+    edge_same = (d, 3 * side)
+
+    def chunk(j):
+        return pl.ds(pl.multiple_of(j * CH, CH), CH)
+
+    def rows_of(q):
+        return pl.ds(pl.multiple_of(q * QT, QT), QT)
+
+    fast = jnp.where(c == 0, x, y)
+    slow = jnp.where(c == 0, y, x)
+    share = c * 16 + slow * 4 + fast
+
+    def share_copy(w):
+        dest = far if w == 0 else near
+        rows = pl.ds(pl.multiple_of(share * WR, WR), WR)
+        return remote(w_hbm.at[rows, slab(dest)], wx.at[w, c, slow, fast], shs.at[w], shr.at[w], mid_same)
+
+    def line_peer(i, fast_axis):
+        along_x = (c == 0) if fast_axis else (c == 1)
+        return (jnp.where(along_x, xpeer[i][0], ypeer[i][0]), k)
+
     z1 = remote(qall.at[y, zh], qall.at[y, zh], ms.at[0], mr.at[0], partner)
     z1.start()
+
+    @pl.when(edge)
+    def _():
+        share_copy(0).start()
+
     loads[1].wait()
     loads[2].wait()
     px = [
@@ -137,94 +180,91 @@
         attn[:, cols] = (dot(w.astype(BF16), values) / total).astype(BF16)
         return 0
 
-    lax.fori_loop(0, GROUP, one_head, 0)
-    loads[3].wait()
-
-    edge = (k == 0) | (k == 3)
-    mid = (k == 1) | (k == 2)
-    side = k // 2
-    mid_same = (d, 1 + side)
-    mid_other = (d, 2 - side)
-    edge_same = (d, 3 * side)
-
-    def first_dest(p):
-        return jnp.where(side == 0, 3 - p, p)
-
-    def edge_copy(p, j):
-        return remote(outP.at[p, j], inP.at[p, j], outPs.at[p, j], inPr.at[p, j], mid_same)
-
-    def mid_copy(p, j):
-        return remote(outP.at[p, j], inS.at[p, j], outPs.at[p, j], inSr.at[p, j], mid_other)
+    lax.fori_loop(0, GROUP, one_head, 0, unroll=True)
+
+    def gather_fast(w):
+        return [
+            remote(wx.at[w, c, slow, fast], wx.at[w, c, slow, fast], gfs.at[w, i], gfr.at[w, i], line_peer(i, True))
+            for i in range(3)
+        ]
+
+    def gather_slow(w):
+        return [
+            remote(wx.at[w, c, slow], wx.at[w, c, slow], gss.at[w, i], gsr.at[w, i], line_peer(i, False))
+            for i in range(3)
+        ]
+
+    def gather_core(w):
+        return [remote(wx.at[w, c], wx.at[w, c], gcs.at[w], gcr.at[w], sibling)]
+
+    def start(copies):
+        for copy in copies:
+            copy.start()
+
+    def wait(copies):
+        for copy in copies:
+            copy.wait()
+
+    def edge_copy(j):
+        return remote(outP.at[j], inP.at[j], outPs.at[j], inPr.at[j], mid_same)
+
+    def rows_copy(q):
+        return remote(attn.at[rows_of(q)], far_attn.at[rows_of(q)], outAs.at[q], inAr.at[q], mid_same)
+
+    def mid_copy(j):
+        return remote(outP.at[j], inS.at[j], outPs.at[j], inSr.at[j], mid_other)
 
     def back_copy(j):
-        return remote(outS.at[j], inS.at[0, j], outSs.at[j], inSr.at[0, j], edge_same)
-
-    def cols_of(dest, j):
-        return pl.ds(pl.multiple_of(dest * SHARD + j * CH, CH), CH)
-
-    def first(p, j):
-        tmp[...] = dot(attn[...], wv[:, cols_of(first_dest(p), j)])
-
+        return remote(outS.at[j], inS.at[j], outSs.at[j], inSr.at[j], edge_same)
+
+    def cross_copy(q):
+        return remote(outQ.at[q], inQ.at[q], outQs.at[q], inQr.at[q], mid_other)
+
+    def own_part(i):
+        slabs[i].wait()
+        own[i] = dot(attn[...], wv[i])
+
+    def first(j):
         @pl.when(mid)
         def _():
-            edge_copy(p, j).wait_recv()
-            tmp[...] += inP[p, j].astype(F32)
-
-        outP[p, j] = tmp[...].astype(BF16)
+            edge_copy(j).wait_recv()
+            outP[j] = (own[0, :, chunk(j)] + inP[j].astype(F32)).astype(BF16)
+            mid_copy(j).start()
 
         @pl.when(edge)
         def _():
-            edge_copy(p, j).start()
-
+            outP[j] = own[0, :, chunk(j)].astype(BF16)
+            edge_copy(j).start()
+
+    def second(j):
         @pl.when(mid)
         def _():
-            mid_copy(p, j).start()
-
-    def second(j):
-        tmp[...] = dot(attn[...], wv[:, cols_of(3 * side, j)])
-        mid_copy(0, j).wait_recv()
-        outS[j] = (tmp[...] + inS[0, j].astype(F32)).astype(BF16)
-        back_copy(j).start()
-
-    def final(j):
-        tmp[...] = dot(attn[...], wv[:, cols_of(k, j)])
-
+            mid_copy(j).wait_recv()
+            outS[j] = (own[1, :, chunk(j)] + inS[j].astype(F32)).astype(BF16)
+            back_copy(j).start()
+
+    def quarter(q):
         @pl.when(mid)
         def _():
-            edge_copy(2, j).wait_recv()
-            mid_copy(1, j).wait_recv()
-            tmp[...] += inP[2, j].astype(F32) + inS[1, j].astype(F32)
-
+            rows_copy(q).wait_recv()
+            part = dot(far_attn[rows_of(q), :], wx[0].reshape(1024, SHARD))
+            outQ[q] = (own[2, rows_of(q), :] + part).astype(BF16)
+            cross_copy(q).start()
+
+    def far_part():
+        own[3] += dot(far_attn[...], wx[1].reshape(1024, SHARD))
+
+    def mid_final(q):
+        @pl.when(mid)
+        def _():
+            cross_copy(q).wait_recv()
+            pout_ref[rows_of(q), :] = (own[3, rows_of(q), :] + inQ[q].astype(F32)).astype(BF16)
+
+    def edge_final(j):
         @pl.when(edge)
         def _():
             back_copy(j).wait_recv()
-            tmp[...] += inS[0, j].astype(F32)
-
-        pout_ref[:, pl.ds(pl.multiple_of(j * CH, CH), CH)] = tmp[...].astype(BF16)
-
-    def items(lo, hi):
-        def body(n, _):
-            p, j = n // NCH, lax.rem(n, NCH)
-
-            @pl.when(edge & (n >= 2))
-            def _():
-                edge_copy((n - 2) // NCH, lax.rem(n - 2, NCH)).wait_send()
-
-            @pl.when(edge | (n < 2 * NCH))
-            def _():
-                first(p, j)
-
-            @pl.when(mid & (n >= 1) & (n <= NCH))
-            def _():
-                second(n - 1)
-
-            @pl.when(n >= 2 * NCH)
-            def _():
-                final(n - 2 * NCH)
-
-            return 0
-
-        lax.fori_loop(lo, hi, body, 0)
+            pout_ref[:, chunk(j)] = (own[1, :, chunk(j)] + inS[j].astype(F32)).astype(BF16)
 
     def dedge_copy(p):
         return remote(doutP.at[p], dinP.at[p], doutPs.at[p], dinPr.at[p], mid_same)
@@ -235,59 +275,46 @@
     def dback_copy():
         return remote(doutS, dinS.at[0], doutSs.at[0], dinSr.at[0], edge_same)
 
-    def ddot(dest):
-        def tile(j, _):
-            out = pl.ds(pl.multiple_of(j * CH, CH), CH)
-            dtmp[:, out] = dot(dattn[...], wv[:, cols_of(dest, j)])
-            return 0
-
-        lax.fori_loop(0, NCH, tile, 0)
+    def dot_all():
+        for i in range(4):
+            down[i] = dot(dattn[...], wv[i])
 
     def dfirst(p):
-        ddot(first_dest(p))
+        i = (0, 2, 3)[p]
 
         @pl.when(mid)
         def _():
             dedge_copy(p).wait_recv()
-            dtmp[...] += dinP[p].astype(F32)
-
-        doutP[p] = dtmp[...].astype(BF16)
+            doutP[p] = (down[i] + dinP[p].astype(F32)).astype(BF16)
+            dmid_copy(p).start()
 
         @pl.when(edge)
         def _():
+            doutP[p] = down[i].astype(BF16)
             dedge_copy(p).start()
 
-        @pl.when(mid)
-        def _():
-            dmid_copy(p).start()
-
     def dsecond():
-        ddot(3 * side)
         dmid_copy(0).wait_recv()
-        doutS[...] = (dtmp[...] + dinS[0].astype(F32)).astype(BF16)
+        doutS[...] = (down[1] + dinS[0].astype(F32)).astype(BF16)
         dback_copy().start()
 
     def dfinal():
-        ddot(k)
-
         @pl.when(mid)
         def _():
             dedge_copy(2).wait_recv()
             dmid_copy(1).wait_recv()
-            dtmp[...] += dinP[2].astype(F32) + dinS[1].astype(F32)
+            dout_ref[...] = (down[3] + dinP[2].astype(F32) + dinS[1].astype(F32)).astype(BF16)
 
         @pl.when(edge)
         def _():
             dback_copy().wait_recv()
-            dtmp[...] += dinS[0].astype(F32)
-
-        dout_ref[...] = dtmp[...].astype(BF16)
+            dout_ref[...] = (down[1] + dinS[0].astype(F32)).astype(BF16)
 
     rmod = lax.rem(lax.broadcasted_iota(jnp.int32, (128, 128), 0), SAMPLES)
     lane128 = lax.broadcasted_iota(jnp.int32, (128, 128), 1)
 
     def suffix():
-        loads[4].wait()
+        loads[3].wait()
         qs = stack_heads(dq_ref[...])
         scores = jnp.zeros((128, 128), F32)
         lens = jnp.zeros((128, 128), jnp.int32)
@@ -323,7 +350,7 @@
         number = tags[:, 0:1] * 16.0 + tags[:, 1:2] - (a * 128).astype(F32)
         to_slot = jnp.where(number == lane128.astype(F32), 1.0, 0.0)
         qsel[...] = dot(to_slot.T.astype(BF16), rows[:, 0:1024]).astype(BF16)
-        lane16 = lax.broadcasted_iota(jnp.int32, (SAMPLES, 128), 1)
+        head128 = lax.broadcasted_iota(jnp.int32, (128, 128), 0) // SAMPLES
 
         def one_prompt(j, _):
             slot = pl.ds(pl.multiple_of(j * SAMPLES, SAMPLES), SAMPLES)
@@ -341,11 +368,8 @@
             total = jnp.sum(w, axis=1, keepdims=True)
             o = dot(w.astype(BF16), v_) / total
             osel[slot, 0:1024] = unstack_heads(o).astype(BF16)
-            stat = jnp.zeros((SAMPLES, 128), F32)
-            for h in range(GROUP):
-                rows_h = slice(SAMPLES * h, SAMPLES * (h + 1))
-                stat = jnp.where(lane16 == h, top[rows_h], stat)
-                stat = jnp.where(lane16 == GROUP + h, total[rows_h], stat)
+            stat = jnp.where(lane128 == head128, top, jnp.where(lane128 == head128 + GROUP, total, 0.0))
+            stat = sum(stat[SAMPLES * h : SAMPLES * (h + 1)] for h in range(GROUP))
             hi = stat.astype(BF16).astype(F32)
             mid = (stat - hi).astype(BF16).astype(F32)
             lo = (stat - hi - mid).astype(BF16).astype(F32)
@@ -353,7 +377,7 @@
             osel[slot, 1024:MSG] = packed.astype(BF16)
             return 0
 
-        lax.fori_loop(0, 8, one_prompt, 0)
+        lax.fori_loop(0, 8, one_prompt, 0, unroll=4)
         back = dot(to_slot.astype(BF16), osel[...]).astype(BF16)
         rsend[...] = back.reshape(4, 2, SAMPLES, MSG)
 
@@ -385,67 +409,123 @@
             + rrecv[2, 1 - zh].astype(F32)
         ).astype(BF16)
 
-    items(0, 1)
+    def on_mid(f, *args):
+        @pl.when(mid)
+        def _():
+            f(*args)
+
+    def own_mid():
+        own[2] = dot(attn[...], wv[2])
+        own[3] = dot(attn[...], wv[3])
+
+    def on_edge(f, *args):
+        @pl.when(edge)
+        def _():
+            f(*args)
+
+    def share_arrived(w):
+        share_copy(w).wait_recv()
+        start(gather_fast(w))
+
+    def fast_done(w):
+        wait(gather_fast(w))
+        start(gather_slow(w))
+
+    def slow_done(w):
+        wait(gather_slow(w))
+        start(gather_core(w))
+
+    own_part(0)
+    on_mid(share_arrived, 0)
+    first(0)
+    own_part(1)
     z1.wait()
-    for copy in y1:
-        copy.start()
+    start(y1)
+    first(1)
+    on_edge(lambda: share_copy(1).start())
     suffix()
-    items(1, 4)
-    for copy in px:
-        copy.wait()
+    on_mid(fast_done, 0)
+    slabs[2].wait()
+    slabs[3].wait()
+    on_edge(lambda: edge_copy(0).wait_send())
+    first(2)
+    second(0)
+    on_mid(own_mid)
+    on_mid(share_arrived, 1)
+    on_edge(lambda: edge_copy(1).wait_send())
+    first(3)
+    second(1)
+    wait(px)
     core.start()
-    for copy in y1:
-        copy.wait()
-    items(4, 5)
+    wait(y1)
+    on_edge(lambda: edge_copy(2).wait_send())
+    first(4)
+    second(2)
+    on_mid(slow_done, 0)
     core.wait()
+    on_edge(lambda: edge_copy(3).wait_send())
+    on_edge(lambda: rows_copy(0).start())
     prefix()
-    for copy in y2:
-        copy.start()
-    items(5, 7)
-    for copy in y2:
-        copy.wait()
+    start(y2)
+    second(3)
+    on_mid(fast_done, 1)
+    on_edge(lambda: edge_copy(4).wait_send())
+    on_edge(lambda: rows_copy(1).start())
+    on_mid(lambda: wait(gather_core(0)))
+    quarter(0)
+    second(4)
+    on_edge(lambda: rows_copy(0).wait_send())
+    on_edge(lambda: rows_copy(2).start())
+    wait(y2)
     sum_for_partner()
     z2.start()
-    items(7, 9)
+    quarter(1)
+    on_edge(lambda: rows_copy(1).wait_send())
+    on_edge(lambda: rows_copy(3).start())
+    for j in range(NCH):
+        edge_final(j)
+    quarter(2)
+    on_mid(slow_done, 1)
     z2.wait()
     merge()
+    dot_all()
     dfirst(0)
-    items(9, 11)
     dfirst(1)
+    on_edge(lambda: dfirst(2))
+    quarter(3)
+    on_mid(dsecond)
+    on_mid(lambda: wait(gather_core(1)))
+    on_mid(far_part)
+    mid_final(0)
+    mid_final(1)
+    mid_final(2)
+    dfinal()
+    mid_final(3)
+
+    @pl.when(edge)
+    def _():
+        share_copy(0).wait_send()
+        share_copy(1).wait_send()
+        rows_copy(2).wait_send()
+        rows_copy(3).wait_send()
+        for p in range(3):
+            dedge_copy(p).wait_send()
 
     @pl.when(mid)
     def _():
-        dsecond()
-
-    items(11, 13)
-
-    @pl.when(edge)
-    def _():
-        dfirst(2)
-
-    items(13, 14)
-    dfinal()
-    items(14, 15)
-
-    @pl.when(edge)
-    def _():
-        edge_copy(2, NCH - 2).wait_send()
-        edge_copy(2, NCH - 1).wait_send()
-        for p in range(3):
-            dedge_copy(p).wait_send()
-
-    @pl.when(mid)
-    def _():
-        def done(j, _):
-            mid_copy(0, j).wait_send()
-            mid_copy(1, j).wait_send()
+        for j in range(NCH):
+            mid_copy(j).wait_send()
             back_copy(j).wait_send()
-            return 0
-
-        lax.fori_loop(0, NCH, done, 0)
+        for q in range(4):
+            cross_copy(q).wait_send()
         dmid_copy(0).wait_send()
         dmid_copy(1).wait_send()
         dback_copy().wait_send()
+
+
+def hand_over(a_ref, b_ref, a_out, b_out):
+    a_out[...] = a_ref[...]
+    b_out[...] = b_ref[...]
 
 
 def local(
@@ -463,7 +543,7 @@
     def dring(*lead):
         return pltpu.VMEM(lead + (SAMPLES, SHARD), BF16)
 
-    return pl.pallas_call(
+    results = pl.pallas_call(
         kernel,
         out_shape=(
             jax.ShapeDtypeStruct((SAMPLES, SHARD), BF16),
@@ -472,7 +552,7 @@
         in_specs=[smem] * 3 + [vmem] * 4 + [hbm] * 4,
         out_specs=(vmem, vmem),
         scratch_shapes=[
-            pltpu.VMEM((1024, 4 * SHARD), BF16),
+            pltpu.VMEM((4, 1024, SHARD), BF16),
             pltpu.VMEM((256, 1024), BF16),
             pltpu.VMEM((SAMPLES, 2, 128, 128), BF16),
             pltpu.VMEM((2, 4, KVROWS, HD), BF16),
@@ -483,18 +563,23 @@
             pltpu.VMEM((SAMPLES, MSG), BF16),
             pltpu.VMEM((256, 1024), BF16),
             pltpu.VMEM((SAMPLES, 1024), BF16),
-            pltpu.VMEM((256, CH), F32),
-            pltpu.VMEM((SAMPLES, SHARD), F32),
+            pltpu.VMEM((4, 256, SHARD), F32),
+            pltpu.VMEM((4, SAMPLES, SHARD), F32),
             pltpu.VMEM((256, 256), F32),
             pltpu.VMEM((128, 1024), BF16),
             pltpu.VMEM((128, MSG), BF16),
             pltpu.VMEM((128, 128), F32),
             pltpu.VMEM((128, 128), F32),
             pltpu.VMEM((128, 128), F32),
-            ring(3, NCH), ring(3, NCH), ring(NCH), ring(2, NCH),
+            pltpu.VMEM((2, 2, 4, 4, WR, SHARD), BF16),
+            pltpu.VMEM((256, 1024), BF16),
+            ring(NCH), ring(NCH), ring(NCH), ring(NCH),
+            pltpu.VMEM((4, QT, SHARD), BF16),
+            pltpu.VMEM((4, QT, SHARD), BF16),
             dring(3), dring(3), dring(), dring(2),
-            dma((5,)), dma((3,)), dma((3,)), dma((3,)), dma((3,)), dma((3,)), dma((3,)), dma((3,)), dma((3,)),
-            dma((3, NCH)), dma((3, NCH)), dma((NCH,)), dma((2, NCH)),
+            dma((8,)), dma((3,)), dma((3,)), dma((3,)), dma((3,)), dma((3,)), dma((3,)), dma((3,)), dma((3,)),
+            dma((2,)), dma((2,)), dma((2, 3)), dma((2, 3)), dma((2, 3)), dma((2, 3)), dma((2,)), dma((2,)),
+            dma((NCH,)), dma((NCH,)), dma((NCH,)), dma((NCH,)), dma((4,)), dma((4,)), dma((4,)), dma((4,)),
             dma((3,)), dma((3,)), dma((1,)), dma((2,)),
         ],
         compiler_params=pltpu.CompilerParams(
@@ -504,6 +589,12 @@
         sample_order, suffix_len, prefix_len, decode_query, new_kv, prefill_kv, prefill_segment,
         prefill_query, suffix_kv, prefix_kv, out_weight,
     )
+    return pl.pallas_call(
+        hand_over,
+        out_shape=tuple(jax.ShapeDtypeStruct(r.shape, r.dtype) for r in results),
+        in_specs=[vmem, vmem],
+        out_specs=(vmem, vmem),
+    )(*results)
 
 
 def solution(mesh):

time: 67.6 us -> 62.4 us (0.923)
  local copies, waits for them, and re-layouts: 3.36 us -> 0 us
  Pallas kernels: 62.8 us -> 60.7 us
    pallas_call x1, Pallas kernels: 62.8 us -> 58.7 us  [local(): pl.pallas_call(kernel, out_shape=(jax.ShapeDtypeStruct((SAMPLES, SHARD),...]
    unnamed x2 -> x0, local copies, waits for them, and re-layouts: 3.36 us -> none
    pallas_call x0 -> x1, Pallas kernels: none -> 2 us  [local(): pl.pallas_call(hand_over, out_shape=tuple((jax.ShapeDtypeStruct(r.shape,...]
where the time goes in v3:
time: 62.4 us; the launch traced here: 62 us
  Pallas kernels  60.7 us (97%)
  between operations  1.29 us (2%)
    pallas_call x1, Pallas kernels, local(): pl.pallas_call(kernel, out_shape=(jax.ShapeDtypeStruct((SAMPLES, SHARD),...  58.7 us
    pallas_call x1, Pallas kernels, local(): pl.pallas_call(hand_over, out_shape=tuple((jax.ShapeDtypeStruct(r.shape,...  2 us

profile of v3, /device:TPU:32, one launch (start us, length us, event | category | flops | bytes accessed | tf_op | source)
XLA Modules:
  0.0 62.0 jit_solution(18272184970317657027)
XLA Ops:
  1.3 58.7 %shard_map.122 = (bf16[16,1280]{1,0:T(8,128)(2,1)}, bf16[256,1280]{1,0:T(8,128)(2,1)}) custom-call(s32[16]{0:T(128)} %so_ref.1, s32[16]{0:T(128)} %sl_ref.1, s32[1]{0:T(128)S(6)} %copy.13.pfl_ref, bf16[16,1024]{1,0:T(8,128)(2,1)} %dq_ref.1, bf16[16,2,128]{2,1,0:T(2,128)(2,1)} %nkv_ref.1, bf16[256,2,128]{2,1,0:T(2,128)(2,1)} %pkv_ref.1, s32[1,256]{1,0:T(1,128)} %seg_ref.1, ...), custom_call_target="tpu_custom_call" | custom-call | tf_op jit(solution)/shard_map/pallas_call | solution.py:546
  60.0 2.0 %shard_map.123 = (bf16[16,1280]{1,0:T(8,128)(2,1)}, bf16[256,1280]{1,0:T(8,128)(2,1)}) custom-call(bf16[16,1280]{1,0:T(8,128)(2,1)} %get-tuple-element.4.a_ref, bf16[256,1280]{1,0:T(8,128)(2,1)} %get-tuple-element.5.b_ref), custom_call_target="tpu_custom_call" | custom-call | tf_op jit(solution)/shard_map/pallas_call | solution.py:592

commit v4 on v3

--- a/solution.py
+++ b/solution.py
@@ -16,10 +16,12 @@
 PX = 384
 MSG = 1024 + 128
 KVROWS = 2 * PX + 16
-CH = 256
-NCH = 5
+CH = 128
+NCH = 10
 SHARD = CH * NCH
 QT = 64
+EX = 2
+FAR = SHARD - EX * CH
 WR = 32
 F32 = jnp.float32
 BF16 = jnp.bfloat16
@@ -42,15 +44,17 @@
 
 
 def kernel(
-    so_ref, sl_ref, pfl_ref, dq_ref, nkv_ref, pkv_ref, seg_ref, pq_hbm, skv_hbm, pre_hbm, w_hbm,
-    dout_ref, pout_ref,
-    wv, pq, skv, pall, qall, rsend, rrecv, zsend, zrecv,
+    so_ref, sl_ref, pfl_ref, dq_hbm, nkv_hbm, pkv_hbm, seg_hbm, pq_hbm, skv_hbm, pre_hbm, w_hbm,
+    dout_hbm, pout_hbm,
+    dout_ref, pout_ref, osem,
+    wv, dq_ref, nkv_ref, pkv_ref, seg_ref, pq, skv, pall, qall, rsend, rrecv, zsend, zrecv,
     attn, dattn, own, down, bias, qsel, osel, suf_o, suf_m, suf_l,
-    wx, far_attn, outP, inP, outS, inS, outQ, inQ, doutP, dinP, doutS, dinS,
+    wx_far, wx_near, far_attn, outP, inP, outS, inS, outQ, inQ, down_out, down_in,
     lsem, xs, xr, ys, yr, y2s, y2r, ms, mr,
     shs, shr, gfs, gfr, gss, gsr, gcs, gcr,
-    outPs, inPr, outSs, inSr, outAs, inAr, outQs, inQr, doutPs, dinPr, doutSs, dinSr,
+    outPs, inPr, outSs, inSr, outAs, inAr, outQs, inQr, downs, downr,
 ):
+    wx = (wx_far, wx_near)
     d = lax.axis_index("dp")
     k = lax.axis_index("head")
     c = lax.rem(d, 2)
@@ -66,20 +70,13 @@
     partner = dev(y, 1 - zh, x, c)
     xpeer = [dev(y, zh, lax.rem(x + i, 4), c) for i in (1, 2, 3)]
     ypeer = [dev(lax.rem(y + i, 4), zh, x, c) for i in (1, 2, 3)]
-    right = (d, jnp.minimum(k + 1, 3))
-    left = (d, jnp.maximum(k - 1, 0))
 
     bar = pltpu.get_barrier_semaphore()
     for peer in [sibling, partner] + xpeer + ypeer:
         pl.semaphore_signal(bar, inc=1, device_id=peer, device_id_type=MESH)
 
-    @pl.when(k < 3)
-    def _():
-        pl.semaphore_signal(bar, inc=1, device_id=right, device_id_type=MESH)
-
-    @pl.when(k > 0)
-    def _():
-        pl.semaphore_signal(bar, inc=1, device_id=left, device_id_type=MESH)
+    for i in (1, 2, 3):
+        pl.semaphore_signal(bar, inc=1, device_id=(d, lax.rem(k + i, 4)), device_id_type=MESH)
 
     loads = [
         pltpu.make_async_copy(pq_hbm, pq, lsem.at[0]),
@@ -98,7 +95,13 @@
     slabs = [
         pltpu.make_async_copy(w_hbm.at[:, slab(role_dest[i])], wv.at[i], lsem.at[4 + i]) for i in range(4)
     ]
-    for load in [loads[0], loads[1], loads[2], slabs[0], loads[3]] + slabs[1:]:
+    small = [
+        pltpu.make_async_copy(dq_hbm, dq_ref, lsem.at[8]),
+        pltpu.make_async_copy(pkv_hbm, pkv_ref, lsem.at[9]),
+        pltpu.make_async_copy(seg_hbm, seg_ref, lsem.at[10]),
+        pltpu.make_async_copy(nkv_hbm, nkv_ref, lsem.at[11]),
+    ]
+    for load in small + [loads[0], loads[1], loads[2], slabs[0], loads[3]] + slabs[1:]:
         load.start()
 
     lane = lax.broadcasted_iota(jnp.int32, (SAMPLES, 128), 1)
@@ -108,6 +111,7 @@
         number = so_ref[r]
         part = jnp.where(lane == 0, number >> 4, jnp.where(lane == 1, number & 15, 0))
         extra = jnp.where(row == r, part, extra)
+    small[0].wait()
     qall[y, zh, :, 0:1024] = dq_ref[...]
     qall[y, zh, :, 1024:MSG] = extra.astype(F32).astype(BF16)
     length = pfl_ref[0]
@@ -115,7 +119,7 @@
         jnp.where(row == 0, length >> 4, jnp.where(row == 1, length & 15, 0)).astype(F32).astype(BF16)
     )
 
-    pl.semaphore_wait(bar, 8 + jnp.where(k < 3, 1, 0) + jnp.where(k > 0, 1, 0))
+    pl.semaphore_wait(bar, 11)
 
     def remote(src, dst, ss, rs, target):
         return pltpu.make_async_remote_copy(
@@ -139,9 +143,12 @@
     share = c * 16 + slow * 4 + fast
 
     def share_copy(w):
-        dest = far if w == 0 else near
         rows = pl.ds(pl.multiple_of(share * WR, WR), WR)
-        return remote(w_hbm.at[rows, slab(dest)], wx.at[w, c, slow, fast], shs.at[w], shr.at[w], mid_same)
+        if w == 0:
+            cols = pl.ds(pl.multiple_of(far * SHARD + EX * CH, CH), FAR)
+        else:
+            cols = slab(near)
+        return remote(w_hbm.at[rows, cols], wx[w].at[c, slow, fast], shs.at[w], shr.at[w], mid_same)
 
     def line_peer(i, fast_axis):
         along_x = (c == 0) if fast_axis else (c == 1)
@@ -159,9 +166,16 @@
     px = [
         remote(pall.at[c, x], pall.at[c, x], xs.at[i], xr.at[i], xpeer[i]) for i in range(3)
     ]
-    for copy in px:
-        copy.start()
-
+
+    @pl.when(edge | (c == 1))
+    def _():
+        for copy in px:
+            copy.start()
+
+
+    small[1].wait()
+    small[2].wait()
+    small[3].wait()
     qpos = lax.broadcasted_iota(jnp.int32, (256, 256), 0)
     kpos = lax.broadcasted_iota(jnp.int32, (256, 256), 1)
     seg_row = jnp.broadcast_to(seg_ref[...].astype(F32), (256, 256))
@@ -184,18 +198,18 @@
 
     def gather_fast(w):
         return [
-            remote(wx.at[w, c, slow, fast], wx.at[w, c, slow, fast], gfs.at[w, i], gfr.at[w, i], line_peer(i, True))
+            remote(wx[w].at[c, slow, fast], wx[w].at[c, slow, fast], gfs.at[w, i], gfr.at[w, i], line_peer(i, True))
             for i in range(3)
         ]
 
     def gather_slow(w):
         return [
-            remote(wx.at[w, c, slow], wx.at[w, c, slow], gss.at[w, i], gsr.at[w, i], line_peer(i, False))
+            remote(wx[w].at[c, slow], wx[w].at[c, slow], gss.at[w, i], gsr.at[w, i], line_peer(i, False))
             for i in range(3)
         ]
 
     def gather_core(w):
-        return [remote(wx.at[w, c], wx.at[w, c], gcs.at[w], gcr.at[w], sibling)]
+        return [remote(wx[w].at[c], wx[w].at[c], gcs.at[w], gcr.at[w], sibling)]
 
     def start(copies):
         for copy in copies:
@@ -224,16 +238,19 @@
         slabs[i].wait()
         own[i] = dot(attn[...], wv[i])
 
+    def own_first(j):
+        return own[0, :, chunk(j)] if j < NCH else own[2, :, chunk(j - NCH)]
+
     def first(j):
         @pl.when(mid)
         def _():
             edge_copy(j).wait_recv()
-            outP[j] = (own[0, :, chunk(j)] + inP[j].astype(F32)).astype(BF16)
+            outP[j] = (own_first(j) + inP[j].astype(F32)).astype(BF16)
             mid_copy(j).start()
 
         @pl.when(edge)
         def _():
-            outP[j] = own[0, :, chunk(j)].astype(BF16)
+            outP[j] = own_first(j).astype(BF16)
             edge_copy(j).start()
 
     def second(j):
@@ -247,18 +264,44 @@
         @pl.when(mid)
         def _():
             rows_copy(q).wait_recv()
-            part = dot(far_attn[rows_of(q), :], wx[0].reshape(1024, SHARD))
-            outQ[q] = (own[2, rows_of(q), :] + part).astype(BF16)
+            part = dot(far_attn[rows_of(q), :], wx_far[...].reshape(1024, FAR))
+            outQ[q] = (own[2, rows_of(q), EX * CH : SHARD] + part).astype(BF16)
             cross_copy(q).start()
 
     def far_part():
-        own[3] += dot(far_attn[...], wx[1].reshape(1024, SHARD))
+        own[3] += dot(far_attn[...], wx_near[...].reshape(1024, SHARD))
+
+    far_cols = pl.ds(EX * CH, FAR)
+
+    def quarter_home(q):
+        return pltpu.make_async_copy(
+            pout_ref.at[rows_of(q), far_cols], pout_hbm.at[rows_of(q), far_cols], osem.at[q]
+        )
+
+    def first_home():
+        cols = pl.ds(0, EX * CH)
+        return pltpu.make_async_copy(pout_ref.at[:, cols], pout_hbm.at[:, cols], osem.at[4])
+
+    def all_home():
+        return pltpu.make_async_copy(pout_ref, pout_hbm, osem.at[5])
+
+    def decode_home():
+        return pltpu.make_async_copy(dout_ref, dout_hbm, osem.at[6])
 
     def mid_final(q):
         @pl.when(mid)
         def _():
             cross_copy(q).wait_recv()
-            pout_ref[rows_of(q), :] = (own[3, rows_of(q), :] + inQ[q].astype(F32)).astype(BF16)
+            cols = slice(EX * CH, SHARD)
+            pout_ref[rows_of(q), cols] = (own[3, rows_of(q), cols] + inQ[q].astype(F32)).astype(BF16)
+            quarter_home(q).start()
+
+    def mid_final_first(j):
+        @pl.when(mid)
+        def _():
+            mid_copy(j).wait_recv()
+            cols = chunk(j - NCH)
+            pout_ref[:, cols] = (own[3, :, cols] + inS[j].astype(F32)).astype(BF16)
 
     def edge_final(j):
         @pl.when(edge)
@@ -266,49 +309,42 @@
             back_copy(j).wait_recv()
             pout_ref[:, chunk(j)] = (own[1, :, chunk(j)] + inS[j].astype(F32)).astype(BF16)
 
-    def dedge_copy(p):
-        return remote(doutP.at[p], dinP.at[p], doutPs.at[p], dinPr.at[p], mid_same)
-
-    def dmid_copy(p):
-        return remote(doutP.at[p], dinS.at[p], doutPs.at[p], dinSr.at[p], mid_other)
-
-    def dback_copy():
-        return remote(doutS, dinS.at[0], doutSs.at[0], dinSr.at[0], edge_same)
-
-    def dot_all():
+    def row_copy(i):
+        return remote(down_out.at[i], down_in.at[k], downs.at[i], downr.at[k], (d, role_dest[i]))
+
+    def row_from(j):
+        return remote(down_out.at[0], down_in.at[j], downs.at[0], downr.at[j], (d, j))
+
+    def decode_out(i):
+        down[i] = dot(dattn[...], wv[i])
+
+        @pl.when(role_dest[i] != k)
+        def _():
+            down_out[i] = down[i].astype(BF16)
+            row_copy(i).start()
+
+    def decode_final():
+        on_edge(lambda: down_sum(down[1]))
+        on_mid(lambda: down_sum(down[3]))
+        for j in range(4):
+
+            @pl.when(k != j)
+            def _():
+                row_from(j).wait_recv()
+                down[4] += down_in[j].astype(F32)
+
+        dout_ref[...] = down[4].astype(BF16)
+        decode_home().start()
+
+    def down_sum(value):
+        down[4] = value
+
+    def decode_sent():
         for i in range(4):
-            down[i] = dot(dattn[...], wv[i])
-
-    def dfirst(p):
-        i = (0, 2, 3)[p]
-
-        @pl.when(mid)
-        def _():
-            dedge_copy(p).wait_recv()
-            doutP[p] = (down[i] + dinP[p].astype(F32)).astype(BF16)
-            dmid_copy(p).start()
-
-        @pl.when(edge)
-        def _():
-            doutP[p] = down[i].astype(BF16)
-            dedge_copy(p).start()
-
-    def dsecond():
-        dmid_copy(0).wait_recv()
-        doutS[...] = (down[1] + dinS[0].astype(F32)).astype(BF16)
-        dback_copy().start()
-
-    def dfinal():
-        @pl.when(mid)
-        def _():
-            dedge_copy(2).wait_recv()
-            dmid_copy(1).wait_recv()
-            dout_ref[...] = (down[3] + dinP[2].astype(F32) + dinS[1].astype(F32)).astype(BF16)
-
-        @pl.when(edge)
-        def _():
-            dback_copy().wait_recv()
-            dout_ref[...] = (down[1] + dinS[0].astype(F32)).astype(BF16)
+
+            @pl.when(role_dest[i] != k)
+            def _():
+                row_copy(i).wait_send()
 
     rmod = lax.rem(lax.broadcasted_iota(jnp.int32, (128, 128), 0), SAMPLES)
     lane128 = lax.broadcasted_iota(jnp.int32, (128, 128), 1)
@@ -344,12 +380,16 @@
     ]
     z2 = remote(zsend, zrecv, ms.at[2], mr.at[2], partner)
 
-    def prefix():
-        rows = qall[...].reshape(128, MSG)
-        tags = rows[:, 1024:MSG].astype(F32)
+    def to_slots():
+        tags = qall[:, :, :, 1024:MSG].reshape(128, 128).astype(F32)
         number = tags[:, 0:1] * 16.0 + tags[:, 1:2] - (a * 128).astype(F32)
-        to_slot = jnp.where(number == lane128.astype(F32), 1.0, 0.0)
-        qsel[...] = dot(to_slot.T.astype(BF16), rows[:, 0:1024]).astype(BF16)
+        return jnp.where(number == lane128.astype(F32), 1.0, 0.0)
+
+    def prefix_begin():
+        rows = qall[:, :, :, 0:1024].reshape(128, 1024)
+        qsel[...] = dot(to_slots().T.astype(BF16), rows).astype(BF16)
+
+    def prefix_part(lo, hi):
         head128 = lax.broadcasted_iota(jnp.int32, (128, 128), 0) // SAMPLES
 
         def one_prompt(j, _):
@@ -370,15 +410,17 @@
             osel[slot, 0:1024] = unstack_heads(o).astype(BF16)
             stat = jnp.where(lane128 == head128, top, jnp.where(lane128 == head128 + GROUP, total, 0.0))
             stat = sum(stat[SAMPLES * h : SAMPLES * (h + 1)] for h in range(GROUP))
-            hi = stat.astype(BF16).astype(F32)
-            mid = (stat - hi).astype(BF16).astype(F32)
-            lo = (stat - hi - mid).astype(BF16).astype(F32)
-            packed = hi + pltpu.roll(mid, 16, 1) + pltpu.roll(lo, 32, 1)
+            hi_ = stat.astype(BF16).astype(F32)
+            mid_ = (stat - hi_).astype(BF16).astype(F32)
+            lo_ = (stat - hi_ - mid_).astype(BF16).astype(F32)
+            packed = hi_ + pltpu.roll(mid_, 16, 1) + pltpu.roll(lo_, 32, 1)
             osel[slot, 1024:MSG] = packed.astype(BF16)
             return 0
 
-        lax.fori_loop(0, 8, one_prompt, 0, unroll=4)
-        back = dot(to_slot.astype(BF16), osel[...]).astype(BF16)
+        lax.fori_loop(lo, hi, one_prompt, 0, unroll=True)
+
+    def prefix_end():
+        back = dot(to_slots().astype(BF16), osel[...]).astype(BF16)
         rsend[...] = back.reshape(4, 2, SAMPLES, MSG)
 
     def merge():
@@ -435,92 +477,128 @@
         wait(gather_slow(w))
         start(gather_core(w))
 
+    def firsts(j):
+        first(2 * j)
+        first(2 * j + 1)
+
+    def seconds(j):
+        second(2 * j)
+        second(2 * j + 1)
+
+    def on_mid_core(i, f, *args):
+        @pl.when(mid & (c == i))
+        def _():
+            f(*args)
+
+    def own_far():
+        own[2] = dot(attn[...], wv[2])
+
+    def own_near():
+        own[3] = dot(attn[...], wv[3])
+
     own_part(0)
+    on_edge(firsts, 0)
+    on_edge(firsts, 1)
     on_mid(share_arrived, 0)
-    first(0)
+    on_mid_core(0, start, px)
     own_part(1)
     z1.wait()
     start(y1)
-    first(1)
+    suffix()
+    on_edge(firsts, 2)
     on_edge(lambda: share_copy(1).start())
-    suffix()
-    on_mid(fast_done, 0)
     slabs[2].wait()
     slabs[3].wait()
-    on_edge(lambda: edge_copy(0).wait_send())
-    first(2)
-    second(0)
-    on_mid(own_mid)
-    on_mid(share_arrived, 1)
-    on_edge(lambda: edge_copy(1).wait_send())
-    first(3)
-    second(1)
+    on_mid(firsts, 0)
+    own_far()
+    on_mid(own_near)
+    on_mid_core(0, fast_done, 0)
+    on_edge(firsts, 3)
+    on_mid(firsts, 1)
     wait(px)
     core.start()
     wait(y1)
-    on_edge(lambda: edge_copy(2).wait_send())
-    first(4)
-    second(2)
-    on_mid(slow_done, 0)
+    prefix_begin()
+    on_mid(firsts, 2)
+    seconds(0)
     core.wait()
-    on_edge(lambda: edge_copy(3).wait_send())
+    on_mid_core(1, fast_done, 0)
+    on_mid(firsts, 3)
+    on_edge(firsts, 4)
+    prefix_part(0, 8)
+    prefix_end()
+    start(y2)
+    on_edge(firsts, 5)
     on_edge(lambda: rows_copy(0).start())
-    prefix()
-    start(y2)
-    second(3)
-    on_mid(fast_done, 1)
-    on_edge(lambda: edge_copy(4).wait_send())
-    on_edge(lambda: rows_copy(1).start())
-    on_mid(lambda: wait(gather_core(0)))
-    quarter(0)
-    second(4)
-    on_edge(lambda: rows_copy(0).wait_send())
-    on_edge(lambda: rows_copy(2).start())
+    on_mid(share_arrived, 1)
+    on_mid(firsts, 4)
+    seconds(1)
+    on_mid_core(0, slow_done, 0)
+    seconds(2)
+    on_mid(firsts, 5)
+    on_mid_core(0, fast_done, 1)
     wait(y2)
     sum_for_partner()
     z2.start()
+    on_edge(lambda: rows_copy(1).start())
+    on_edge(lambda: rows_copy(2).start())
+    on_edge(lambda: rows_copy(3).start())
+    on_mid_core(1, slow_done, 0)
+    on_mid_core(1, fast_done, 1)
+    seconds(3)
+    on_mid(lambda: wait(gather_core(0)))
+    quarter(0)
+    seconds(4)
     quarter(1)
-    on_edge(lambda: rows_copy(1).wait_send())
-    on_edge(lambda: rows_copy(3).start())
+    z2.wait()
+    merge()
+    decode_out(0)
+    decode_out(2)
+    decode_out(3)
+    decode_out(1)
+    on_mid_core(0, slow_done, 1)
+    quarter(2)
+    on_mid_core(1, slow_done, 1)
+    quarter(3)
     for j in range(NCH):
         edge_final(j)
-    quarter(2)
-    on_mid(slow_done, 1)
-    z2.wait()
-    merge()
-    dot_all()
-    dfirst(0)
-    dfirst(1)
-    on_edge(lambda: dfirst(2))
-    quarter(3)
-    on_mid(dsecond)
+    on_edge(lambda: all_home().start())
     on_mid(lambda: wait(gather_core(1)))
     on_mid(far_part)
+    for j in range(NCH, NCH + EX):
+        mid_final_first(j)
+    on_mid(lambda: first_home().start())
     mid_final(0)
     mid_final(1)
     mid_final(2)
-    dfinal()
+    decode_final()
     mid_final(3)
+
+    decode_home().wait()
 
     @pl.when(edge)
     def _():
+        all_home().wait()
         share_copy(0).wait_send()
         share_copy(1).wait_send()
-        rows_copy(2).wait_send()
-        rows_copy(3).wait_send()
-        for p in range(3):
-            dedge_copy(p).wait_send()
+        for j in range(NCH + EX):
+            edge_copy(j).wait_send()
+        for q in range(4):
+            rows_copy(q).wait_send()
 
     @pl.when(mid)
     def _():
+        first_home().wait()
+        for q in range(4):
+            quarter_home(q).wait()
+        for j in range(NCH + EX):
+            mid_copy(j).wait_send()
         for j in range(NCH):
-            mid_copy(j).wait_send()
             back_copy(j).wait_send()
         for q in range(4):
             cross_copy(q).wait_send()
-        dmid_copy(0).wait_send()
-        dmid_copy(1).wait_send()
-        dback_copy().wait_send()
+
+    decode_sent()
 
 
 def hand_over(a_ref, b_ref, a_out, b_out):
@@ -549,10 +627,17 @@
             jax.ShapeDtypeStruct((SAMPLES, SHARD), BF16),
             jax.ShapeDtypeStruct((256, SHARD), BF16),
         ),
-        in_specs=[smem] * 3 + [vmem] * 4 + [hbm] * 4,
-        out_specs=(vmem, vmem),
+        in_specs=[smem] * 3 + [hbm] * 8,
+        out_specs=(hbm, hbm),
         scratch_shapes=[
+            pltpu.VMEM((SAMPLES, SHARD), BF16),
+            pltpu.VMEM((256, SHARD), BF16),
+            dma((9,)),
             pltpu.VMEM((4, 1024, SHARD), BF16),
+            pltpu.VMEM(decode_query.shape, BF16),
+            pltpu.VMEM(new_kv.shape, BF16),
+            pltpu.VMEM(prefill_kv.shape, BF16),
+            pltpu.VMEM(prefill_segment.shape, jnp.int32),
             pltpu.VMEM((256, 1024), BF16),
             pltpu.VMEM((SAMPLES, 2, 128, 128), BF16),
             pltpu.VMEM((2, 4, KVROWS, HD), BF16),
@@ -564,23 +649,24 @@
             pltpu.VMEM((256, 1024), BF16),
             pltpu.VMEM((SAMPLES, 1024), BF16),
             pltpu.VMEM((4, 256, SHARD), F32),
-            pltpu.VMEM((4, SAMPLES, SHARD), F32),
+            pltpu.VMEM((5, SAMPLES, SHARD), F32),
             pltpu.VMEM((256, 256), F32),
             pltpu.VMEM((128, 1024), BF16),
             pltpu.VMEM((128, MSG), BF16),
             pltpu.VMEM((128, 128), F32),
             pltpu.VMEM((128, 128), F32),
             pltpu.VMEM((128, 128), F32),
-            pltpu.VMEM((2, 2, 4, 4, WR, SHARD), BF16),
+            pltpu.VMEM((2, 4, 4, WR, FAR), BF16),
+            pltpu.VMEM((2, 4, 4, WR, SHARD), BF16),
             pltpu.VMEM((256, 1024), BF16),
-            ring(NCH), ring(NCH), ring(NCH), ring(NCH),
-            pltpu.VMEM((4, QT, SHARD), BF16),
-            pltpu.VMEM((4, QT, SHARD), BF16),
-            dring(3), dring(3), dring(), dring(2),
-            dma((8,)), dma((3,)), dma((3,)), dma((3,)), dma((3,)), dma((3,)), dma((3,)), dma((3,)), dma((3,)),
+            ring(NCH + EX), ring(NCH + EX), ring(NCH), ring(NCH + EX),
+            pltpu.VMEM((4, QT, FAR), BF16),
+            pltpu.VMEM((4, QT, FAR), BF16),
+            dring(4), dring(4),
+            dma((12,)), dma((3,)), dma((3,)), dma((3,)), dma((3,)), dma((3,)), dma((3,)), dma((3,)), dma((3,)),
             dma((2,)), dma((2,)), dma((2, 3)), dma((2, 3)), dma((2, 3)), dma((2, 3)), dma((2,)), dma((2,)),
-            dma((NCH,)), dma((NCH,)), dma((NCH,)), dma((NCH,)), dma((4,)), dma((4,)), dma((4,)), dma((4,)),
-            dma((3,)), dma((3,)), dma((1,)), dma((2,)),
+            dma((NCH + EX,)), dma((NCH + EX,)), dma((NCH,)), dma((NCH + EX,)), dma((4,)), dma((4,)), dma((4,)), dma((4,)),
+            dma((4,)), dma((4,)),
         ],
         compiler_params=pltpu.CompilerParams(
             collective_id=0, has_side_effects=True, vmem_limit_bytes=60 << 20

time: 62.4 us -> 58.8 us (0.942)
  Pallas kernels: 60.7 us -> 57.4 us
    pallas_call x1, Pallas kernels: 58.7 us -> 55.4 us  [local(): pl.pallas_call(kernel, out_shape=(jax.ShapeDtypeStruct((SAMPLES, SHARD),...]
where the time goes in v4:
time: 58.8 us; the launch traced here: 58.7 us
  Pallas kernels  57.4 us (98%)
  between operations  1.29 us (2%)
    pallas_call x1, Pallas kernels, local(): pl.pallas_call(kernel, out_shape=(jax.ShapeDtypeStruct((SAMPLES, SHARD),...  55.4 us
    pallas_call x1, Pallas kernels, local(): pl.pallas_call(hand_over, out_shape=tuple((jax.ShapeDtypeStruct(r.shape,...  2 us

profile of v4, /device:TPU:32, one launch (start us, length us, event | category | flops | bytes accessed | tf_op | source)
XLA Modules:
  0.0 58.7 jit_solution(6017167097062222335)
XLA Ops:
  1.3 55.4 %shard_map.122 = (bf16[16,1280]{1,0:T(8,128)(2,1)}, bf16[256,1280]{1,0:T(8,128)(2,1)}) custom-call(s32[16]{0:T(128)} %so_ref.1, s32[16]{0:T(128)} %sl_ref.1, s32[1]{0:T(128)S(6)} %copy.13.pfl_ref, bf16[16,1024]{1,0:T(8,128)(2,1)} %dq_hbm.1, bf16[16,2,128]{2,1,0:T(2,128)(2,1)} %nkv_hbm.1, bf16[256,2,128]{2,1,0:T(2,128)(2,1)} %pkv_hbm.1, s32[1,256]{1,0:T(1,128)} %seg_hbm.1, ...), custom_call_target="tpu_custom_call" | custom-call | tf_op jit(solution)/shard_map/pallas_call | solution.py:624
  56.7 2.0 %shard_map.123 = (bf16[16,1280]{1,0:T(8,128)(2,1)}, bf16[256,1280]{1,0:T(8,128)(2,1)}) custom-call(bf16[16,1280]{1,0:T(8,128)(2,1)} %get-tuple-element.4.a_ref, bf16[256,1280]{1,0:T(8,128)(2,1)} %get-tuple-element.5.b_ref), custom_call_target="tpu_custom_call" | custom-call | tf_op jit(solution)/shard_map/pallas_call | solution.py:678

commit v5 on v4

--- a/solution.py
+++ b/solution.py
@@ -19,7 +19,8 @@
 CH = 128
 NCH = 10
 SHARD = CH * NCH
-QT = 64
+QT = 32
+NQ = 8
 EX = 2
 FAR = SHARD - EX * CH
 WR = 32
@@ -104,6 +105,48 @@
     for load in small + [loads[0], loads[1], loads[2], slabs[0], loads[3]] + slabs[1:]:
         load.start()
 
+    pl.semaphore_wait(bar, 11)
+
+
+    def remote(src, dst, ss, rs, target):
+        return pltpu.make_async_remote_copy(
+            src_ref=src, dst_ref=dst, send_sem=ss, recv_sem=rs, device_id=target, device_id_type=MESH
+        )
+
+    edge = (k == 0) | (k == 3)
+    mid = (k == 1) | (k == 2)
+    mid_same = (d, 1 + side)
+    mid_other = (d, 2 - side)
+    edge_same = (d, 3 * side)
+
+    def chunk(j):
+        return pl.ds(pl.multiple_of(j * CH, CH), CH)
+
+    def rows_of(q):
+        return pl.ds(pl.multiple_of(q * QT, QT), QT)
+
+    fast = jnp.where(c == 0, x, y)
+    slow = jnp.where(c == 0, y, x)
+    share = c * 16 + slow * 4 + fast
+
+    def share_copy(w):
+        rows = pl.ds(pl.multiple_of(share * WR, WR), WR)
+        if w == 0:
+            cols = pl.ds(pl.multiple_of(far * SHARD + EX * CH, CH), FAR)
+        else:
+            cols = slab(near)
+        return remote(w_hbm.at[rows, cols], wx[w].at[c, slow, fast], shs.at[w], shr.at[w], mid_same)
+
+    def line_peer(i, fast_axis):
+        along_x = (c == 0) if fast_axis else (c == 1)
+        return (jnp.where(along_x, xpeer[i][0], ypeer[i][0]), k)
+
+    z1 = remote(qall.at[y, zh], qall.at[y, zh], ms.at[0], mr.at[0], partner)
+
+    @pl.when(edge)
+    def _():
+        share_copy(0).start()
+
     lane = lax.broadcasted_iota(jnp.int32, (SAMPLES, 128), 1)
     row = lax.broadcasted_iota(jnp.int32, (SAMPLES, 128), 0)
     extra = jnp.zeros((SAMPLES, 128), jnp.int32)
@@ -119,48 +162,7 @@
         jnp.where(row == 0, length >> 4, jnp.where(row == 1, length & 15, 0)).astype(F32).astype(BF16)
     )
 
-    pl.semaphore_wait(bar, 11)
-
-    def remote(src, dst, ss, rs, target):
-        return pltpu.make_async_remote_copy(
-            src_ref=src, dst_ref=dst, send_sem=ss, recv_sem=rs, device_id=target, device_id_type=MESH
-        )
-
-    edge = (k == 0) | (k == 3)
-    mid = (k == 1) | (k == 2)
-    mid_same = (d, 1 + side)
-    mid_other = (d, 2 - side)
-    edge_same = (d, 3 * side)
-
-    def chunk(j):
-        return pl.ds(pl.multiple_of(j * CH, CH), CH)
-
-    def rows_of(q):
-        return pl.ds(pl.multiple_of(q * QT, QT), QT)
-
-    fast = jnp.where(c == 0, x, y)
-    slow = jnp.where(c == 0, y, x)
-    share = c * 16 + slow * 4 + fast
-
-    def share_copy(w):
-        rows = pl.ds(pl.multiple_of(share * WR, WR), WR)
-        if w == 0:
-            cols = pl.ds(pl.multiple_of(far * SHARD + EX * CH, CH), FAR)
-        else:
-            cols = slab(near)
-        return remote(w_hbm.at[rows, cols], wx[w].at[c, slow, fast], shs.at[w], shr.at[w], mid_same)
-
-    def line_peer(i, fast_axis):
-        along_x = (c == 0) if fast_axis else (c == 1)
-        return (jnp.where(along_x, xpeer[i][0], ypeer[i][0]), k)
-
-    z1 = remote(qall.at[y, zh], qall.at[y, zh], ms.at[0], mr.at[0], partner)
     z1.start()
-
-    @pl.when(edge)
-    def _():
-        share_copy(0).start()
-
     loads[1].wait()
     loads[2].wait()
     px = [
@@ -280,13 +282,13 @@
 
     def first_home():
         cols = pl.ds(0, EX * CH)
-        return pltpu.make_async_copy(pout_ref.at[:, cols], pout_hbm.at[:, cols], osem.at[4])
+        return pltpu.make_async_copy(pout_ref.at[:, cols], pout_hbm.at[:, cols], osem.at[NQ])
 
     def all_home():
-        return pltpu.make_async_copy(pout_ref, pout_hbm, osem.at[5])
+        return pltpu.make_async_copy(pout_ref, pout_hbm, osem.at[NQ + 1])
 
     def decode_home():
-        return pltpu.make_async_copy(dout_ref, dout_hbm, osem.at[6])
+        return pltpu.make_async_copy(dout_ref, dout_hbm, osem.at[NQ + 2])
 
     def mid_final(q):
         @pl.when(mid)
@@ -309,42 +311,50 @@
             back_copy(j).wait_recv()
             pout_ref[:, chunk(j)] = (own[1, :, chunk(j)] + inS[j].astype(F32)).astype(BF16)
 
-    def row_copy(i):
-        return remote(down_out.at[i], down_in.at[k], downs.at[i], downr.at[k], (d, role_dest[i]))
-
-    def row_from(j):
-        return remote(down_out.at[0], down_in.at[j], downs.at[0], downr.at[j], (d, j))
+    def row_copy(i, slot, target):
+        return remote(down_out.at[i], down_in.at[slot], downs.at[i], downr.at[slot], target)
+
+    def row_from_edge(i):
+        return row_copy(i, (0, 0, 1, 2)[i], mid_same)
+
+    def row_to_edge():
+        return row_copy(1, 3, edge_same)
+
+    def row_across(i):
+        return row_copy(i, 4, (d, role_dest[i]))
 
     def decode_out(i):
         down[i] = dot(dattn[...], wv[i])
 
-        @pl.when(role_dest[i] != k)
+        @pl.when(edge & (i != 1))
         def _():
             down_out[i] = down[i].astype(BF16)
-            row_copy(i).start()
+            row_from_edge(i).start()
+
+        @pl.when(mid & (i == 1))
+        def _():
+            down_out[1] = down[1].astype(BF16)
+            row_to_edge().start()
+
+    def decode_across(i):
+        row_from_edge(i).wait_recv()
+        down_out[i] = (down[i] + down_in[(0, 0, 1, 2)[i]].astype(F32)).astype(BF16)
+        row_across(i).start()
 
     def decode_final():
-        on_edge(lambda: down_sum(down[1]))
-        on_mid(lambda: down_sum(down[3]))
-        for j in range(4):
-
-            @pl.when(k != j)
-            def _():
-                row_from(j).wait_recv()
-                down[4] += down_in[j].astype(F32)
-
-        dout_ref[...] = down[4].astype(BF16)
+        @pl.when(mid)
+        def _():
+            row_from_edge(3).wait_recv()
+            row_across(2).wait_recv()
+            dout_ref[...] = (down[3] + down_in[2].astype(F32) + down_in[4].astype(F32)).astype(BF16)
+
+        @pl.when(edge)
+        def _():
+            row_to_edge().wait_recv()
+            row_across(0).wait_recv()
+            dout_ref[...] = (down[1] + down_in[3].astype(F32) + down_in[4].astype(F32)).astype(BF16)
+
         decode_home().start()
-
-    def down_sum(value):
-        down[4] = value
-
-    def decode_sent():
-        for i in range(4):
-
-            @pl.when(role_dest[i] != k)
-            def _():
-                row_copy(i).wait_send()
 
     rmod = lax.rem(lax.broadcasted_iota(jnp.int32, (128, 128), 0), SAMPLES)
     lane128 = lax.broadcasted_iota(jnp.int32, (128, 128), 1)
@@ -478,8 +488,9 @@
         start(gather_core(w))
 
     def firsts(j):
-        first(2 * j)
-        first(2 * j + 1)
+        for i in (2 * j, 2 * j + 1):
+            if i < NCH + EX:
+                first(i)
 
     def seconds(j):
         second(2 * j)
@@ -496,24 +507,35 @@
     def own_near():
         own[3] = dot(attn[...], wv[3])
 
+    def rows_out(lo, hi):
+        for q in range(lo, hi):
+            rows_copy(q).start()
+
+    def sent_early():
+        for j in range(NCH + EX):
+            mid_copy(j).wait_send()
+        for j in range(NCH):
+            back_copy(j).wait_send()
+
     own_part(0)
     on_edge(firsts, 0)
+    on_edge(lambda: share_copy(1).start())
     on_edge(firsts, 1)
     on_mid(share_arrived, 0)
     on_mid_core(0, start, px)
     own_part(1)
     z1.wait()
     start(y1)
+    on_edge(firsts, 2)
     suffix()
-    on_edge(firsts, 2)
-    on_edge(lambda: share_copy(1).start())
     slabs[2].wait()
     slabs[3].wait()
     on_mid(firsts, 0)
     own_far()
-    on_mid(own_near)
+    on_mid(share_arrived, 1)
     on_mid_core(0, fast_done, 0)
     on_edge(firsts, 3)
+    on_mid(own_near)
     on_mid(firsts, 1)
     wait(px)
     core.start()
@@ -521,45 +543,53 @@
     prefix_begin()
     on_mid(firsts, 2)
     seconds(0)
+    on_mid_core(1, fast_done, 0)
     core.wait()
-    on_mid_core(1, fast_done, 0)
+    on_edge(firsts, 4)
+    prefix_part(0, 4)
     on_mid(firsts, 3)
-    on_edge(firsts, 4)
-    prefix_part(0, 8)
+    prefix_part(4, 8)
     prefix_end()
     start(y2)
     on_edge(firsts, 5)
-    on_edge(lambda: rows_copy(0).start())
-    on_mid(share_arrived, 1)
+    on_edge(firsts, 6)
+    on_edge(rows_out, 0, 2)
     on_mid(firsts, 4)
     seconds(1)
     on_mid_core(0, slow_done, 0)
+    on_mid_core(0, fast_done, 1)
     seconds(2)
     on_mid(firsts, 5)
-    on_mid_core(0, fast_done, 1)
+    on_mid_core(1, slow_done, 0)
+    on_mid_core(1, fast_done, 1)
+    on_mid(firsts, 6)
     wait(y2)
     sum_for_partner()
     z2.start()
-    on_edge(lambda: rows_copy(1).start())
-    on_edge(lambda: rows_copy(2).start())
-    on_edge(lambda: rows_copy(3).start())
-    on_mid_core(1, slow_done, 0)
-    on_mid_core(1, fast_done, 1)
+    on_edge(rows_out, 2, 6)
     seconds(3)
     on_mid(lambda: wait(gather_core(0)))
     quarter(0)
+    quarter(1)
     seconds(4)
-    quarter(1)
+    quarter(2)
+    quarter(3)
     z2.wait()
     merge()
     decode_out(0)
     decode_out(2)
     decode_out(3)
+    on_edge(rows_out, 6, 8)
+    quarter(4)
+    on_mid_core(0, slow_done, 1)
     decode_out(1)
-    on_mid_core(0, slow_done, 1)
-    quarter(2)
+    quarter(5)
     on_mid_core(1, slow_done, 1)
-    quarter(3)
+    on_mid(decode_across, 0)
+    on_mid(decode_across, 2)
+    quarter(6)
+    on_mid(sent_early)
+    quarter(7)
     for j in range(NCH):
         edge_final(j)
     on_edge(lambda: all_home().start())
@@ -568,11 +598,10 @@
     for j in range(NCH, NCH + EX):
         mid_final_first(j)
     on_mid(lambda: first_home().start())
-    mid_final(0)
-    mid_final(1)
-    mid_final(2)
+    for q in range(NQ - 1):
+        mid_final(q)
     decode_final()
-    mid_final(3)
+    mid_final(NQ - 1)
 
     decode_home().wait()
 
@@ -583,27 +612,37 @@
         share_copy(1).wait_send()
         for j in range(NCH + EX):
             edge_copy(j).wait_send()
-        for q in range(4):
+        for q in range(NQ):
             rows_copy(q).wait_send()
+        for i in (0, 2, 3):
+            row_from_edge(i).wait_send()
 
     @pl.when(mid)
     def _():
         first_home().wait()
-        for q in range(4):
+        for q in range(NQ):
             quarter_home(q).wait()
-        for j in range(NCH + EX):
-            mid_copy(j).wait_send()
-        for j in range(NCH):
-            back_copy(j).wait_send()
-        for q in range(4):
             cross_copy(q).wait_send()
-
-    decode_sent()
-
-
-def hand_over(a_ref, b_ref, a_out, b_out):
-    a_out[...] = a_ref[...]
-    b_out[...] = b_ref[...]
+        row_across(0).wait_send()
+        row_across(2).wait_send()
+        row_to_edge().wait_send()
+
+
+def hand_over(a_hbm, b_hbm, a_out, b_out, a_vmem, b_vmem, in_sems, out_sems):
+    rows = b_vmem.shape[0] // 4
+    parts = [(a_hbm, a_vmem, a_out)]
+    for i in range(4):
+        part = pl.ds(i * rows, rows)
+        parts.append((b_hbm.at[part], b_vmem.at[part], b_out.at[part]))
+    inward = [pltpu.make_async_copy(p[0], p[1], in_sems.at[i]) for i, p in enumerate(parts)]
+    outward = [pltpu.make_async_copy(p[1], p[2], out_sems.at[i]) for i, p in enumerate(parts)]
+    for copy in inward:
+        copy.start()
+    for come, go in zip(inward, outward):
+        come.wait()
+        go.start()
+    for copy in outward:
+        copy.wait()
 
 
 def local(
@@ -632,7 +671,7 @@
         scratch_shapes=[
             pltpu.VMEM((SAMPLES, SHARD), BF16),
             pltpu.VMEM((256, SHARD), BF16),
-            dma((9,)),
+            dma((NQ + 3,)),
             pltpu.VMEM((4, 1024, SHARD), BF16),
             pltpu.VMEM(decode_query.shape, BF16),
             pltpu.VMEM(new_kv.shape, BF16),
@@ -649,7 +688,7 @@
             pltpu.VMEM((256, 1024), BF16),
             pltpu.VMEM((SAMPLES, 1024), BF16),
             pltpu.VMEM((4, 256, SHARD), F32),
-            pltpu.VMEM((5, SAMPLES, SHARD), F32),
+            pltpu.VMEM((4, SAMPLES, SHARD), F32),
             pltpu.VMEM((256, 256), F32),
             pltpu.VMEM((128, 1024), BF16),
             pltpu.VMEM((128, MSG), BF16),
@@ -660,13 +699,13 @@
             pltpu.VMEM((2, 4, 4, WR, SHARD), BF16),
             pltpu.VMEM((256, 1024), BF16),
             ring(NCH + EX), ring(NCH + EX), ring(NCH), ring(NCH + EX),
-            pltpu.VMEM((4, QT, FAR), BF16),
-            pltpu.VMEM((4, QT, FAR), BF16),
-            dring(4), dring(4),
+            pltpu.VMEM((NQ, QT, FAR), BF16),
+            pltpu.VMEM((NQ, QT, FAR), BF16),
+            dring(4), dring(5),
             dma((12,)), dma((3,)), dma((3,)), dma((3,)), dma((3,)), dma((3,)), dma((3,)), dma((3,)), dma((3,)),
             dma((2,)), dma((2,)), dma((2, 3)), dma((2, 3)), dma((2, 3)), dma((2, 3)), dma((2,)), dma((2,)),
-            dma((NCH + EX,)), dma((NCH + EX,)), dma((NCH,)), dma((NCH + EX,)), dma((4,)), dma((4,)), dma((4,)), dma((4,)),
-            dma((4,)), dma((4,)),
+            dma((NCH + EX,)), dma((NCH + EX,)), dma((NCH,)), dma((NCH + EX,)), dma((NQ,)), dma((NQ,)), dma((NQ,)), dma((NQ,)),
+            dma((4,)), dma((5,)),
         ],
         compiler_params=pltpu.CompilerParams(
             collective_id=0, has_side_effects=True, vmem_limit_bytes=60 << 20
@@ -678,8 +717,9 @@
     return pl.pallas_call(
         hand_over,
         out_shape=tuple(jax.ShapeDtypeStruct(r.shape, r.dtype) for r in results),
-        in_specs=[vmem, vmem],
-        out_specs=(vmem, vmem),
+        in_specs=[hbm, hbm],
+        out_specs=(hbm, hbm),
+        scratch_shapes=[pltpu.VMEM(r.shape, r.dtype) for r in results] + [dma((5,)), dma((5,))],
     )(*results)
 
 

time: 58.8 us -> 55.9 us (0.951)
  Pallas kernels: 57.4 us -> 54.2 us
    pallas_call x1, Pallas kernels: 55.4 us -> 52.3 us  [local(): pl.pallas_call(kernel, out_shape=(jax.ShapeDtypeStruct((SAMPLES, SHARD),...]
where the time goes in v5:
time: 55.9 us; the launch traced here: 55.5 us
  Pallas kernels  54.2 us (97%)
  between operations  1.29 us (2%)
    pallas_call x1, Pallas kernels, local(): pl.pallas_call(kernel, out_shape=(jax.ShapeDtypeStruct((SAMPLES, SHARD),...  52.3 us
    pallas_call x1, Pallas kernels, local(): pl.pallas_call(hand_over, out_shape=tuple((jax.ShapeDtypeStruct(r.shape,...  1.93 us

profile of v5, /device:TPU:32, one launch (start us, length us, event | category | flops | bytes accessed | tf_op | source)
XLA Modules:
  0.0 55.5 jit_solution(16332492906401141237)
XLA Ops:
  1.3 52.3 %shard_map.122 = (bf16[16,1280]{1,0:T(8,128)(2,1)}, bf16[256,1280]{1,0:T(8,128)(2,1)}) custom-call(s32[16]{0:T(128)} %so_ref.1, s32[16]{0:T(128)} %sl_ref.1, s32[1]{0:T(128)S(6)} %copy.13.pfl_ref, bf16[16,1024]{1,0:T(8,128)(2,1)} %dq_hbm.1, bf16[16,2,128]{2,1,0:T(2,128)(2,1)} %nkv_hbm.1, bf16[256,2,128]{2,1,0:T(2,128)(2,1)} %pkv_hbm.1, s32[1,256]{1,0:T(1,128)} %seg_hbm.1, ...), custom_call_target="tpu_custom_call" | custom-call | tf_op jit(solution)/shard_map/pallas_call | solution.py:663
  53.6 1.9 %shard_map.123 = (bf16[16,1280]{1,0:T(8,128)(2,1)}, bf16[256,1280]{1,0:T(8,128)(2,1)}) custom-call(bf16[16,1280]{1,0:T(8,128)(2,1)} %get-tuple-element.4.a_hbm, bf16[256,1280]{1,0:T(8,128)(2,1)} %get-tuple-element.5.b_hbm), custom_call_target="tpu_custom_call" | custom-call | tf_op jit(solution)/shard_map/pallas_call | solution.py:717

commit v6 on v5

--- a/solution.py
+++ b/solution.py
@@ -46,8 +46,7 @@
 
 def kernel(
     so_ref, sl_ref, pfl_ref, dq_hbm, nkv_hbm, pkv_hbm, seg_hbm, pq_hbm, skv_hbm, pre_hbm, w_hbm,
-    dout_hbm, pout_hbm,
-    dout_ref, pout_ref, osem,
+    dout_ref, pout_ref,
     wv, dq_ref, nkv_ref, pkv_ref, seg_ref, pq, skv, pall, qall, rsend, rrecv, zsend, zrecv,
     attn, dattn, own, down, bias, qsel, osel, suf_o, suf_m, suf_l,
     wx_far, wx_near, far_attn, outP, inP, outS, inS, outQ, inQ, down_out, down_in,
@@ -166,7 +165,7 @@
     loads[1].wait()
     loads[2].wait()
     px = [
-        remote(pall.at[c, x], pall.at[c, x], xs.at[i], xr.at[i], xpeer[i]) for i in range(3)
+        remote(pall.at[c, x], pall.at[c, x], xs.at[0], xr.at[0], xpeer[i]) for i in range(3)
     ]
 
     @pl.when(edge | (c == 1))
@@ -200,18 +199,37 @@
 
     def gather_fast(w):
         return [
-            remote(wx[w].at[c, slow, fast], wx[w].at[c, slow, fast], gfs.at[w, i], gfr.at[w, i], line_peer(i, True))
+            remote(wx[w].at[c, slow, fast], wx[w].at[c, slow, fast], gfs.at[w], gfr.at[w], line_peer(i, True))
             for i in range(3)
         ]
 
     def gather_slow(w):
         return [
-            remote(wx[w].at[c, slow], wx[w].at[c, slow], gss.at[w, i], gsr.at[w, i], line_peer(i, False))
+            remote(wx[w].at[c, slow], wx[w].at[c, slow], gss.at[w], gsr.at[w], line_peer(i, False))
             for i in range(3)
         ]
 
     def gather_core(w):
         return [remote(wx[w].at[c], wx[w].at[c], gcs.at[w], gcr.at[w], sibling)]
+
+    def fast_all(w):
+        three = wx[w].at[c, slow, pl.ds(0, 3)]
+        return remote(three, three, gfs.at[w], gfr.at[w], line_peer(0, True))
+
+    def slow_all(w):
+        three = wx[w].at[c, pl.ds(0, 3)]
+        return remote(three, three, gss.at[w], gsr.at[w], line_peer(0, False))
+
+    def px_all():
+        three = pall.at[c, pl.ds(0, 3)]
+        return remote(three, three, xs.at[0], xr.at[0], xpeer[0])
+
+    def y1_all():
+        three = qall.at[pl.ds(0, 3)]
+        return remote(three, three, ys.at[0], yr.at[0], ypeer[0])
+
+    def y2_all():
+        return remote(rsend.at[pl.ds(0, 3)], rrecv, y2s.at[0], y2r.at[0], ypeer[0])
 
     def start(copies):
         for copy in copies:
@@ -222,24 +240,31 @@
             copy.wait()
 
     def edge_copy(j):
-        return remote(outP.at[j], inP.at[j], outPs.at[j], inPr.at[j], mid_same)
+        return remote(outP.at[j], inP.at[j], outPs.at[0], inPr.at[j], mid_same)
 
     def rows_copy(q):
-        return remote(attn.at[rows_of(q)], far_attn.at[rows_of(q)], outAs.at[q], inAr.at[q], mid_same)
+        return remote(attn.at[rows_of(q)], far_attn.at[rows_of(q)], outAs.at[0], inAr.at[q], mid_same)
 
     def mid_copy(j):
-        return remote(outP.at[j], inS.at[j], outPs.at[j], inSr.at[j], mid_other)
+        return remote(outP.at[j], inS.at[j], outPs.at[0], inSr.at[j // 2], mid_other)
 
     def back_copy(j):
-        return remote(outS.at[j], inS.at[j], outSs.at[j], inSr.at[j], edge_same)
+        return remote(outS.at[j], inS.at[j], outSs.at[0], inSr.at[j // 2], edge_same)
 
     def cross_copy(q):
-        return remote(outQ.at[q], inQ.at[q], outQs.at[q], inQr.at[q], mid_other)
+        return remote(outQ.at[q], inQ.at[q], outQs.at[0], inQr.at[q], mid_other)
 
     def own_part(i):
         slabs[i].wait()
         own[i] = dot(attn[...], wv[i])
 
+    def own_head():
+        slabs[0].wait()
+        own[0, :, 0 : 2 * CH] = dot(attn[...], wv[0, :, 0 : 2 * CH])
+
+    def own_rest():
+        own[0, :, 2 * CH : SHARD] = dot(attn[...], wv[0, :, 2 * CH : SHARD])
+
     def own_first(j):
         return own[0, :, chunk(j)] if j < NCH else own[2, :, chunk(j - NCH)]
 
@@ -255,12 +280,17 @@
             outP[j] = own_first(j).astype(BF16)
             edge_copy(j).start()
 
-    def second(j):
+    def pair_in(j):
+        two = pl.ds(2 * j, 2)
+        return remote(outP.at[two], inS.at[two], outPs.at[0], inSr.at[j], mid_other)
+
+    def seconds(j):
         @pl.when(mid)
         def _():
-            mid_copy(j).wait_recv()
-            outS[j] = (own[1, :, chunk(j)] + inS[j].astype(F32)).astype(BF16)
-            back_copy(j).start()
+            pair_in(j).wait_recv()
+            for i in (2 * j, 2 * j + 1):
+                outS[i] = (own[1, :, chunk(i)] + inS[i].astype(F32)).astype(BF16)
+                back_copy(i).start()
 
     def quarter(q):
         @pl.when(mid)
@@ -296,23 +326,20 @@
             cross_copy(q).wait_recv()
             cols = slice(EX * CH, SHARD)
             pout_ref[rows_of(q), cols] = (own[3, rows_of(q), cols] + inQ[q].astype(F32)).astype(BF16)
-            quarter_home(q).start()
 
     def mid_final_first(j):
-        @pl.when(mid)
-        def _():
-            mid_copy(j).wait_recv()
-            cols = chunk(j - NCH)
-            pout_ref[:, cols] = (own[3, :, cols] + inS[j].astype(F32)).astype(BF16)
+        pair_in(j).wait_recv()
+        for i in (2 * j, 2 * j + 1):
+            cols = chunk(i - NCH)
+            pout_ref[:, cols] = (own[3, :, cols] + inS[i].astype(F32)).astype(BF16)
 
     def edge_final(j):
-        @pl.when(edge)
-        def _():
-            back_copy(j).wait_recv()
-            pout_ref[:, chunk(j)] = (own[1, :, chunk(j)] + inS[j].astype(F32)).astype(BF16)
+        pair_in(j).wait_recv()
+        for i in (2 * j, 2 * j + 1):
+            pout_ref[:, chunk(i)] = (own[1, :, chunk(i)] + inS[i].astype(F32)).astype(BF16)
 
     def row_copy(i, slot, target):
-        return remote(down_out.at[i], down_in.at[slot], downs.at[i], downr.at[slot], target)
+        return remote(down_out.at[i], down_in.at[slot], downs.at[0], downr.at[slot], target)
 
     def row_from_edge(i):
         return row_copy(i, (0, 0, 1, 2)[i], mid_same)
@@ -353,8 +380,6 @@
             row_to_edge().wait_recv()
             row_across(0).wait_recv()
             dout_ref[...] = (down[1] + down_in[3].astype(F32) + down_in[4].astype(F32)).astype(BF16)
-
-        decode_home().start()
 
     rmod = lax.rem(lax.broadcasted_iota(jnp.int32, (128, 128), 0), SAMPLES)
     lane128 = lax.broadcasted_iota(jnp.int32, (128, 128), 1)
@@ -382,10 +407,10 @@
         suf_m[...] = jnp.broadcast_to(top, (128, 128))
         suf_l[...] = jnp.broadcast_to(jnp.sum(w, axis=1, keepdims=True) + new_w, (128, 128))
 
-    y1 = [remote(qall.at[y], qall.at[y], ys.at[i], yr.at[i], ypeer[i]) for i in range(3)]
+    y1 = [remote(qall.at[y], qall.at[y], ys.at[0], yr.at[0], ypeer[i]) for i in range(3)]
     core = remote(pall.at[c], pall.at[c], ms.at[1], mr.at[1], sibling)
     y2 = [
-        remote(rsend.at[lax.rem(y + i + 1, 4)], rrecv.at[i], y2s.at[i], y2r.at[i], ypeer[i])
+        remote(rsend.at[lax.rem(y + i + 1, 4)], rrecv.at[i], y2s.at[0], y2r.at[0], ypeer[i])
         for i in range(3)
     ]
     z2 = remote(zsend, zrecv, ms.at[2], mr.at[2], partner)
@@ -480,11 +505,11 @@
         start(gather_fast(w))
 
     def fast_done(w):
-        wait(gather_fast(w))
+        fast_all(w).wait()
         start(gather_slow(w))
 
     def slow_done(w):
-        wait(gather_slow(w))
+        slow_all(w).wait()
         start(gather_core(w))
 
     def firsts(j):
@@ -492,10 +517,6 @@
             if i < NCH + EX:
                 first(i)
 
-    def seconds(j):
-        second(2 * j)
-        second(2 * j + 1)
-
     def on_mid_core(i, f, *args):
         @pl.when(mid & (c == i))
         def _():
@@ -512,14 +533,21 @@
             rows_copy(q).start()
 
     def sent_early():
-        for j in range(NCH + EX):
-            mid_copy(j).wait_send()
-        for j in range(NCH):
-            back_copy(j).wait_send()
-
-    own_part(0)
+        remote(outP, inP, outPs.at[0], inPr.at[0], mid_same).wait_send()
+        remote(outS, outS, outSs.at[0], inPr.at[0], mid_same).wait_send()
+
+    def edge_finals():
+        for j in range(NCH // 2):
+            edge_final(j)
+
+    def mid_first_finals():
+        for j in range(NCH // 2, (NCH + EX) // 2):
+            mid_final_first(j)
+
+    own_head()
     on_edge(firsts, 0)
     on_edge(lambda: share_copy(1).start())
+    own_rest()
     on_edge(firsts, 1)
     on_mid(share_arrived, 0)
     on_mid_core(0, start, px)
@@ -537,9 +565,9 @@
     on_edge(firsts, 3)
     on_mid(own_near)
     on_mid(firsts, 1)
-    wait(px)
+    px_all().wait()
     core.start()
-    wait(y1)
+    y1_all().wait()
     prefix_begin()
     on_mid(firsts, 2)
     seconds(0)
@@ -563,7 +591,7 @@
     on_mid_core(1, slow_done, 0)
     on_mid_core(1, fast_done, 1)
     on_mid(firsts, 6)
-    wait(y2)
+    y2_all().wait()
     sum_for_partner()
     z2.start()
     on_edge(rows_out, 2, 6)
@@ -590,59 +618,28 @@
     quarter(6)
     on_mid(sent_early)
     quarter(7)
-    for j in range(NCH):
-        edge_final(j)
-    on_edge(lambda: all_home().start())
+    on_edge(edge_finals)
     on_mid(lambda: wait(gather_core(1)))
     on_mid(far_part)
-    for j in range(NCH, NCH + EX):
-        mid_final_first(j)
-    on_mid(lambda: first_home().start())
+    on_mid(mid_first_finals)
     for q in range(NQ - 1):
         mid_final(q)
     decode_final()
     mid_final(NQ - 1)
 
-    decode_home().wait()
-
     @pl.when(edge)
     def _():
-        all_home().wait()
         share_copy(0).wait_send()
         share_copy(1).wait_send()
-        for j in range(NCH + EX):
-            edge_copy(j).wait_send()
-        for q in range(NQ):
-            rows_copy(q).wait_send()
-        for i in (0, 2, 3):
-            row_from_edge(i).wait_send()
+        remote(outP, inP, outPs.at[0], inPr.at[0], mid_same).wait_send()
+        remote(attn, far_attn, outAs.at[0], inAr.at[0], mid_same).wait_send()
 
     @pl.when(mid)
     def _():
-        first_home().wait()
-        for q in range(NQ):
-            quarter_home(q).wait()
-            cross_copy(q).wait_send()
-        row_across(0).wait_send()
-        row_across(2).wait_send()
-        row_to_edge().wait_send()
-
-
-def hand_over(a_hbm, b_hbm, a_out, b_out, a_vmem, b_vmem, in_sems, out_sems):
-    rows = b_vmem.shape[0] // 4
-    parts = [(a_hbm, a_vmem, a_out)]
-    for i in range(4):
-        part = pl.ds(i * rows, rows)
-        parts.append((b_hbm.at[part], b_vmem.at[part], b_out.at[part]))
-    inward = [pltpu.make_async_copy(p[0], p[1], in_sems.at[i]) for i, p in enumerate(parts)]
-    outward = [pltpu.make_async_copy(p[1], p[2], out_sems.at[i]) for i, p in enumerate(parts)]
-    for copy in inward:
-        copy.start()
-    for come, go in zip(inward, outward):
-        come.wait()
-        go.start()
-    for copy in outward:
-        copy.wait()
+        remote(outQ, inQ, outQs.at[0], inQr.at[0], mid_other).wait_send()
+
+    three = pl.ds(0, 3)
+    remote(down_out.at[three], down_in.at[three], downs.at[0], downr.at[0], mid_same).wait_send()
 
 
 def local(
@@ -660,18 +657,12 @@
     def dring(*lead):
         return pltpu.VMEM(lead + (SAMPLES, SHARD), BF16)
 
-    results = pl.pallas_call(
+    return pl.pallas_call(
         kernel,
-        out_shape=(
-            jax.ShapeDtypeStruct((SAMPLES, SHARD), BF16),
-            jax.ShapeDtypeStruct((256, SHARD), BF16),
-        ),
+        out_shape=(pltpu.VMEM((SAMPLES, SHARD), BF16), pltpu.VMEM((256, SHARD), BF16)),
         in_specs=[smem] * 3 + [hbm] * 8,
-        out_specs=(hbm, hbm),
+        out_specs=(vmem, vmem),
         scratch_shapes=[
-            pltpu.VMEM((SAMPLES, SHARD), BF16),
-            pltpu.VMEM((256, SHARD), BF16),
-            dma((NQ + 3,)),
             pltpu.VMEM((4, 1024, SHARD), BF16),
             pltpu.VMEM(decode_query.shape, BF16),
             pltpu.VMEM(new_kv.shape, BF16),
@@ -702,10 +693,10 @@
             pltpu.VMEM((NQ, QT, FAR), BF16),
             pltpu.VMEM((NQ, QT, FAR), BF16),
             dring(4), dring(5),
-            dma((12,)), dma((3,)), dma((3,)), dma((3,)), dma((3,)), dma((3,)), dma((3,)), dma((3,)), dma((3,)),
-            dma((2,)), dma((2,)), dma((2, 3)), dma((2, 3)), dma((2, 3)), dma((2, 3)), dma((2,)), dma((2,)),
-            dma((NCH + EX,)), dma((NCH + EX,)), dma((NCH,)), dma((NCH + EX,)), dma((NQ,)), dma((NQ,)), dma((NQ,)), dma((NQ,)),
-            dma((4,)), dma((5,)),
+            dma((12,)), dma((1,)), dma((1,)), dma((1,)), dma((1,)), dma((1,)), dma((1,)), dma((3,)), dma((3,)),
+            dma((2,)), dma((2,)), dma((2,)), dma((2,)), dma((2,)), dma((2,)), dma((2,)), dma((2,)),
+            dma((1,)), dma((NCH + EX,)), dma((1,)), dma(((NCH + EX) // 2,)), dma((1,)), dma((NQ,)), dma((1,)), dma((NQ,)),
+            dma((1,)), dma((5,)),
         ],
         compiler_params=pltpu.CompilerParams(
             collective_id=0, has_side_effects=True, vmem_limit_bytes=60 << 20
@@ -714,13 +705,6 @@
         sample_order, suffix_len, prefix_len, decode_query, new_kv, prefill_kv, prefill_segment,
         prefill_query, suffix_kv, prefix_kv, out_weight,
     )
-    return pl.pallas_call(
-        hand_over,
-        out_shape=tuple(jax.ShapeDtypeStruct(r.shape, r.dtype) for r in results),
-        in_specs=[hbm, hbm],
-        out_specs=(hbm, hbm),
-        scratch_shapes=[pltpu.VMEM(r.shape, r.dtype) for r in results] + [dma((5,)), dma((5,))],
-    )(*results)
 
 
 def solution(mesh):

time: 55.9 us -> 54.2 us (0.970)
  Pallas kernels: 54.2 us -> 51.3 us
  local copies, waits for them, and re-layouts: 0 us -> 1.46 us
    pallas_call x2 -> x1, Pallas kernels: 54.2 us -> 51.3 us  [local(): pl.pallas_call(kernel, out_shape=(pltpu.VMEM((SAMPLES, SHARD), BF16), plt...]
    unnamed x0 -> x2, local copies, waits for them, and re-layouts: none -> 1.46 us
where the time goes in v6:
time: 54.2 us; the launch traced here: 54 us
  Pallas kernels  51.3 us (95%)
  local copies, waits for them, and re-layouts  1.46 us (3%)
  between operations  1.29 us (2%)
    pallas_call x1, Pallas kernels, local(): pl.pallas_call(kernel, out_shape=(pltpu.VMEM((SAMPLES, SHARD), BF16), plt...  51.3 us
    unnamed x2, local copies, waits for them, and re-layouts  1.46 us

profile of v6, /device:TPU:32, one launch (start us, length us, event | category | flops | bytes accessed | tf_op | source)
XLA Modules:
  0.0 54.0 jit_solution(17906255673960755854)
XLA Ops:
  1.3 51.3 %shard_map.122 = (bf16[16,1280]{1,0:T(8,128)(2,1)S(1)}, bf16[256,1280]{1,0:T(8,128)(2,1)S(1)}) custom-call(s32[16]{0:T(128)} %so_ref.1, s32[16]{0:T(128)} %sl_ref.1, s32[1]{0:T(128)S(6)} %copy.17.pfl_ref, bf16[16,1024]{1,0:T(8,128)(2,1)} %dq_hbm.1, bf16[16,2,128]{2,1,0:T(2,128)(2,1)} %nkv_hbm.1, bf16[256,2,128]{2,1,0:T(2,128)(2,1)} %pkv_hbm.1, ...), custom_call_target="tpu_custom_call" | custom-call | tf_op jit(solution)/shard_map/pallas_call | solution.py:660
  52.6 0.6 %copy.15 = bf16[16,1280]{1,0:T(8,128)(2,1)} copy(bf16[16,1280]{1,0:T(8,128)(2,1)S(1)} %get-tuple-element.2) | data formatting | bytes 81920
  53.2 0.8 %copy.16 = bf16[256,1280]{1,0:T(8,128)(2,1)} copy(bf16[256,1280]{1,0:T(8,128)(2,1)S(1)} %get-tuple-element.3) | data formatting | bytes 1310720

commit v7 on v6

--- a/solution.py
+++ b/solution.py
@@ -49,8 +49,8 @@
     dout_ref, pout_ref,
     wv, dq_ref, nkv_ref, pkv_ref, seg_ref, pq, skv, pall, qall, rsend, rrecv, zsend, zrecv,
     attn, dattn, own, down, bias, qsel, osel, suf_o, suf_m, suf_l,
-    wx_far, wx_near, far_attn, outP, inP, outS, inS, outQ, inQ, down_out, down_in,
-    lsem, xs, xr, ys, yr, y2s, y2r, ms, mr,
+    wx_far, wx_near, far_attn, outP, inP, outS, inS, outQ, inQ, down_out, down_in, far_dattn, head_out, head_in,
+    half_sem, lsem, xs, xr, ys, yr, y2s, y2r, ms, mr,
     shs, shr, gfs, gfr, gss, gsr, gcs, gcr,
     outPs, inPr, outSs, inSr, outAs, inAr, outQs, inQr, downs, downr,
 ):
@@ -72,8 +72,13 @@
     ypeer = [dev(lax.rem(y + i, 4), zh, x, c) for i in (1, 2, 3)]
 
     bar = pltpu.get_barrier_semaphore()
-    for peer in [sibling, partner] + xpeer + ypeer:
+    for peer in [sibling] + xpeer + ypeer:
         pl.semaphore_signal(bar, inc=1, device_id=peer, device_id_type=MESH)
+
+    @pl.when(zh == 0)
+    def _():
+        pl.semaphore_signal(bar, inc=1, device_id=partner, device_id_type=MESH)
+
 
     for i in (1, 2, 3):
         pl.semaphore_signal(bar, inc=1, device_id=(d, lax.rem(k + i, 4)), device_id_type=MESH)
@@ -104,7 +109,11 @@
     for load in small + [loads[0], loads[1], loads[2], slabs[0], loads[3]] + slabs[1:]:
         load.start()
 
-    pl.semaphore_wait(bar, 11)
+    pl.semaphore_wait(bar, 10 + zh)
+
+    @pl.when(zh == 1)
+    def _():
+        pl.semaphore_signal(half_sem, inc=1, device_id=partner, device_id_type=MESH)
 
 
     def remote(src, dst, ss, rs, target):
@@ -161,7 +170,11 @@
         jnp.where(row == 0, length >> 4, jnp.where(row == 1, length & 15, 0)).astype(F32).astype(BF16)
     )
 
-    z1.start()
+
+    @pl.when(zh == 1)
+    def _():
+        z1.start()
+
     loads[1].wait()
     loads[2].wait()
     px = [
@@ -281,7 +294,7 @@
             edge_copy(j).start()
 
     def pair_in(j):
-        two = pl.ds(2 * j, 2)
+        two = pl.ds(2 * j, min(2, NCH + EX - 2 * j))
         return remote(outP.at[two], inS.at[two], outPs.at[0], inSr.at[j], mid_other)
 
     def seconds(j):
@@ -329,7 +342,7 @@
 
     def mid_final_first(j):
         pair_in(j).wait_recv()
-        for i in (2 * j, 2 * j + 1):
+        for i in range(2 * j, min(2 * j + 2, NCH + EX)):
             cols = chunk(i - NCH)
             pout_ref[:, cols] = (own[3, :, cols] + inS[i].astype(F32)).astype(BF16)
 
@@ -339,10 +352,10 @@
             pout_ref[:, chunk(i)] = (own[1, :, chunk(i)] + inS[i].astype(F32)).astype(BF16)
 
     def row_copy(i, slot, target):
-        return remote(down_out.at[i], down_in.at[slot], downs.at[0], downr.at[slot], target)
-
-    def row_from_edge(i):
-        return row_copy(i, (0, 0, 1, 2)[i], mid_same)
+        return remote(down_out.at[i], down_in.at[slot], downs.at[i], downr.at[slot], target)
+
+    def row_from_edge():
+        return row_copy(0, 0, mid_same)
 
     def row_to_edge():
         return row_copy(1, 3, edge_same)
@@ -350,30 +363,48 @@
     def row_across(i):
         return row_copy(i, 4, (d, role_dest[i]))
 
-    def decode_out(i):
-        down[i] = dot(dattn[...], wv[i])
-
-        @pl.when(edge & (i != 1))
-        def _():
-            down_out[i] = down[i].astype(BF16)
-            row_from_edge(i).start()
-
-        @pl.when(mid & (i == 1))
-        def _():
-            down_out[1] = down[1].astype(BF16)
-            row_to_edge().start()
-
-    def decode_across(i):
-        row_from_edge(i).wait_recv()
-        down_out[i] = (down[i] + down_in[(0, 0, 1, 2)[i]].astype(F32)).astype(BF16)
-        row_across(i).start()
+    def dattn_copy():
+        return remote(dattn, far_dattn, downs.at[3], downr.at[1], mid_same)
+
+    def head_copy():
+        return remote(head_out, head_in, downs.at[4], downr.at[2], mid_same)
+
+    def decode_out_edge():
+        down_out[0] = dot(dattn[...], wv[0]).astype(BF16)
+        row_from_edge().start()
+        dattn_copy().start()
+        head_out[...] = dot(dattn[...], wv[2, :, 0 : EX * CH]).astype(BF16)
+        head_copy().start()
+        down[1] = dot(dattn[...], wv[1])
+
+    def decode_own(i):
+        @pl.when(mid)
+        def _():
+            down[i] = dot(dattn[...], wv[i])
+
+    def decode_to_edge():
+        down_out[1] = dot(dattn[...], wv[1]).astype(BF16)
+        row_to_edge().start()
+
+    def decode_across():
+        row_from_edge().wait_recv()
+        down_out[0] = (down[0] + down_in[0].astype(F32)).astype(BF16)
+        row_across(0).start()
+        dattn_copy().wait_recv()
+        down[2, :, EX * CH : SHARD] += dot(far_dattn[...], wx_far[...].reshape(1024, FAR))
+        head_copy().wait_recv()
+        down[2, :, 0 : EX * CH] += head_in[...].astype(F32)
+        down_out[2] = down[2].astype(BF16)
+        row_across(2).start()
+
+    def decode_near():
+        down[3] += dot(far_dattn[...], wx_near[...].reshape(1024, SHARD))
 
     def decode_final():
         @pl.when(mid)
         def _():
-            row_from_edge(3).wait_recv()
             row_across(2).wait_recv()
-            dout_ref[...] = (down[3] + down_in[2].astype(F32) + down_in[4].astype(F32)).astype(BF16)
+            dout_ref[...] = (down[3] + down_in[4].astype(F32)).astype(BF16)
 
         @pl.when(edge)
         def _():
@@ -541,56 +572,61 @@
             edge_final(j)
 
     def mid_first_finals():
-        for j in range(NCH // 2, (NCH + EX) // 2):
+        for j in range(NCH // 2, (NCH + EX + 1) // 2):
             mid_final_first(j)
+
+    def queries_out():
+        @pl.when(zh == 0)
+        def _():
+            pl.semaphore_wait(half_sem, 1)
+            z1.start()
 
     own_head()
     on_edge(firsts, 0)
     on_edge(lambda: share_copy(1).start())
     own_rest()
-    on_edge(firsts, 1)
     on_mid(share_arrived, 0)
     on_mid_core(0, start, px)
     own_part(1)
-    z1.wait()
-    start(y1)
+    queries_out()
+    on_edge(firsts, 1)
     on_edge(firsts, 2)
+    on_edge(firsts, 3)
     suffix()
     slabs[2].wait()
     slabs[3].wait()
     on_mid(firsts, 0)
     own_far()
+    z1.wait()
+    start(y1)
+    on_edge(firsts, 4)
     on_mid(share_arrived, 1)
     on_mid_core(0, fast_done, 0)
-    on_edge(firsts, 3)
+    on_edge(firsts, 5)
     on_mid(own_near)
     on_mid(firsts, 1)
     px_all().wait()
     core.start()
+    on_mid_core(1, fast_done, 0)
     y1_all().wait()
     prefix_begin()
     on_mid(firsts, 2)
     seconds(0)
-    on_mid_core(1, fast_done, 0)
     core.wait()
-    on_edge(firsts, 4)
     prefix_part(0, 4)
     on_mid(firsts, 3)
     prefix_part(4, 8)
     prefix_end()
     start(y2)
-    on_edge(firsts, 5)
-    on_edge(firsts, 6)
     on_edge(rows_out, 0, 2)
     on_mid(firsts, 4)
     seconds(1)
     on_mid_core(0, slow_done, 0)
     on_mid_core(0, fast_done, 1)
     seconds(2)
-    on_mid(firsts, 5)
     on_mid_core(1, slow_done, 0)
     on_mid_core(1, fast_done, 1)
-    on_mid(firsts, 6)
+    on_mid(firsts, 5)
     y2_all().wait()
     sum_for_partner()
     z2.start()
@@ -602,25 +638,26 @@
     seconds(4)
     quarter(2)
     quarter(3)
+    quarter(4)
+    on_mid_core(0, slow_done, 1)
+    on_mid_core(1, slow_done, 1)
     z2.wait()
     merge()
-    decode_out(0)
-    decode_out(2)
-    decode_out(3)
+    on_edge(decode_out_edge)
     on_edge(rows_out, 6, 8)
-    quarter(4)
-    on_mid_core(0, slow_done, 1)
-    decode_out(1)
+    decode_own(0)
     quarter(5)
-    on_mid_core(1, slow_done, 1)
-    on_mid(decode_across, 0)
-    on_mid(decode_across, 2)
+    decode_own(2)
+    on_mid(decode_to_edge)
+    decode_own(3)
+    on_mid(decode_across)
     quarter(6)
     on_mid(sent_early)
     quarter(7)
     on_edge(edge_finals)
     on_mid(lambda: wait(gather_core(1)))
     on_mid(far_part)
+    on_mid(decode_near)
     on_mid(mid_first_finals)
     for q in range(NQ - 1):
         mid_final(q)
@@ -633,13 +670,16 @@
         share_copy(1).wait_send()
         remote(outP, inP, outPs.at[0], inPr.at[0], mid_same).wait_send()
         remote(attn, far_attn, outAs.at[0], inAr.at[0], mid_same).wait_send()
+        row_from_edge().wait_send()
+        dattn_copy().wait_send()
+        head_copy().wait_send()
 
     @pl.when(mid)
     def _():
         remote(outQ, inQ, outQs.at[0], inQr.at[0], mid_other).wait_send()
-
-    three = pl.ds(0, 3)
-    remote(down_out.at[three], down_in.at[three], downs.at[0], downr.at[0], mid_same).wait_send()
+        row_to_edge().wait_send()
+        row_across(0).wait_send()
+        row_across(2).wait_send()
 
 
 def local(
@@ -692,11 +732,15 @@
             ring(NCH + EX), ring(NCH + EX), ring(NCH), ring(NCH + EX),
             pltpu.VMEM((NQ, QT, FAR), BF16),
             pltpu.VMEM((NQ, QT, FAR), BF16),
-            dring(4), dring(5),
+            dring(3), dring(5),
+            pltpu.VMEM((SAMPLES, 1024), BF16),
+            pltpu.VMEM((SAMPLES, EX * CH), BF16),
+            pltpu.VMEM((SAMPLES, EX * CH), BF16),
+            pltpu.SemaphoreType.REGULAR,
             dma((12,)), dma((1,)), dma((1,)), dma((1,)), dma((1,)), dma((1,)), dma((1,)), dma((3,)), dma((3,)),
             dma((2,)), dma((2,)), dma((2,)), dma((2,)), dma((2,)), dma((2,)), dma((2,)), dma((2,)),
-            dma((1,)), dma((NCH + EX,)), dma((1,)), dma(((NCH + EX) // 2,)), dma((1,)), dma((NQ,)), dma((1,)), dma((NQ,)),
-            dma((1,)), dma((5,)),
+            dma((1,)), dma((NCH + EX,)), dma((1,)), dma(((NCH + EX + 1) // 2,)), dma((1,)), dma((NQ,)), dma((1,)), dma((NQ,)),
+            dma((5,)), dma((5,)),
         ],
         compiler_params=pltpu.CompilerParams(
             collective_id=0, has_side_effects=True, vmem_limit_bytes=60 << 20

time: 54.2 us -> 52.5 us (0.969)
  Pallas kernels: 51.3 us -> 49.6 us
    pallas_call x1, Pallas kernels: 51.3 us -> 49.6 us  [local(): pl.pallas_call(kernel, out_shape=(pltpu.VMEM((SAMPLES, SHARD), BF16), plt...]
where the time goes in v7:
time: 52.5 us; the launch traced here: 52.4 us
  Pallas kernels  49.6 us (94%)
  local copies, waits for them, and re-layouts  1.46 us (3%)
  between operations  1.29 us (2%)
    pallas_call x1, Pallas kernels, local(): pl.pallas_call(kernel, out_shape=(pltpu.VMEM((SAMPLES, SHARD), BF16), plt...  49.6 us
    unnamed x2, local copies, waits for them, and re-layouts  1.46 us

profile of v7, /device:TPU:32, one launch (start us, length us, event | category | flops | bytes accessed | tf_op | source)
XLA Modules:
  0.0 52.4 jit_solution(481508396999084295)
XLA Ops:
  1.3 49.6 %shard_map.122 = (bf16[16,1280]{1,0:T(8,128)(2,1)S(1)}, bf16[256,1280]{1,0:T(8,128)(2,1)S(1)}) custom-call(s32[16]{0:T(128)} %so_ref.1, s32[16]{0:T(128)} %sl_ref.1, s32[1]{0:T(128)S(6)} %copy.17.pfl_ref, bf16[16,1024]{1,0:T(8,128)(2,1)} %dq_hbm.1, bf16[16,2,128]{2,1,0:T(2,128)(2,1)} %nkv_hbm.1, bf16[256,2,128]{2,1,0:T(2,128)(2,1)} %pkv_hbm.1, ...), custom_call_target="tpu_custom_call" | custom-call | tf_op jit(solution)/shard_map/pallas_call | solution.py:700
  50.9 0.6 %copy.15 = bf16[16,1280]{1,0:T(8,128)(2,1)} copy(bf16[16,1280]{1,0:T(8,128)(2,1)S(1)} %get-tuple-element.2) | data formatting | bytes 81920
  51.5 0.8 %copy.16 = bf16[256,1280]{1,0:T(8,128)(2,1)} copy(bf16[256,1280]{1,0:T(8,128)(2,1)S(1)} %get-tuple-element.3) | data formatting | bytes 1310720

commit v8 on v7

--- a/solution.py
+++ b/solution.py
@@ -45,9 +45,9 @@
 
 
 def kernel(
-    so_ref, sl_ref, pfl_ref, dq_hbm, nkv_hbm, pkv_hbm, seg_hbm, pq_hbm, skv_hbm, pre_hbm, w_hbm,
+    so_hbm, sl_hbm, pfl_hbm, dq_hbm, nkv_hbm, pkv_hbm, seg_hbm, pq_hbm, skv_hbm, pre_hbm, w_hbm,
     dout_ref, pout_ref,
-    wv, dq_ref, nkv_ref, pkv_ref, seg_ref, pq, skv, pall, qall, rsend, rrecv, zsend, zrecv,
+    so_ref, sl_ref, pfl_ref, wv, dq_ref, nkv_ref, pkv_ref, seg_ref, pq, skv, pall, qall, rsend, rrecv, zsend, zrecv,
     attn, dattn, own, down, bias, qsel, osel, suf_o, suf_m, suf_l,
     wx_far, wx_near, far_attn, outP, inP, outS, inS, outQ, inQ, down_out, down_in, far_dattn, head_out, head_in,
     half_sem, lsem, xs, xr, ys, yr, y2s, y2r, ms, mr,
@@ -105,6 +105,9 @@
         pltpu.make_async_copy(pkv_hbm, pkv_ref, lsem.at[9]),
         pltpu.make_async_copy(seg_hbm, seg_ref, lsem.at[10]),
         pltpu.make_async_copy(nkv_hbm, nkv_ref, lsem.at[11]),
+        pltpu.make_async_copy(so_hbm, so_ref, lsem.at[12]),
+        pltpu.make_async_copy(pfl_hbm, pfl_ref, lsem.at[13]),
+        pltpu.make_async_copy(sl_hbm, sl_ref, lsem.at[14]),
     ]
     for load in small + [loads[0], loads[1], loads[2], slabs[0], loads[3]] + slabs[1:]:
         load.start()
@@ -155,6 +158,9 @@
     def _():
         share_copy(0).start()
 
+    small[4].wait()
+    small[5].wait()
+    small[6].wait()
     lane = lax.broadcasted_iota(jnp.int32, (SAMPLES, 128), 1)
     row = lax.broadcasted_iota(jnp.int32, (SAMPLES, 128), 0)
     extra = jnp.zeros((SAMPLES, 128), jnp.int32)
@@ -687,7 +693,6 @@
     prefill_query, prefill_kv, prefill_segment, out_weight,
 ):
     vmem = pl.BlockSpec(memory_space=pltpu.VMEM)
-    smem = pl.BlockSpec(memory_space=pltpu.SMEM)
     hbm = pl.BlockSpec(memory_space=pl.ANY)
     dma = pltpu.SemaphoreType.DMA
 
@@ -700,9 +705,12 @@
     return pl.pallas_call(
         kernel,
         out_shape=(pltpu.VMEM((SAMPLES, SHARD), BF16), pltpu.VMEM((256, SHARD), BF16)),
-        in_specs=[smem] * 3 + [hbm] * 8,
+        in_specs=[hbm] * 11,
         out_specs=(vmem, vmem),
         scratch_shapes=[
+            pltpu.SMEM(sample_order.shape, jnp.int32),
+            pltpu.SMEM(suffix_len.shape, jnp.int32),
+            pltpu.SMEM(prefix_len.shape, jnp.int32),
             pltpu.VMEM((4, 1024, SHARD), BF16),
             pltpu.VMEM(decode_query.shape, BF16),
             pltpu.VMEM(new_kv.shape, BF16),
@@ -737,7 +745,7 @@
             pltpu.VMEM((SAMPLES, EX * CH), BF16),
             pltpu.VMEM((SAMPLES, EX * CH), BF16),
             pltpu.SemaphoreType.REGULAR,
-            dma((12,)), dma((1,)), dma((1,)), dma((1,)), dma((1,)), dma((1,)), dma((1,)), dma((3,)), dma((3,)),
+            dma((15,)), dma((1,)), dma((1,)), dma((1,)), dma((1,)), dma((1,)), dma((1,)), dma((3,)), dma((3,)),
             dma((2,)), dma((2,)), dma((2,)), dma((2,)), dma((2,)), dma((2,)), dma((2,)), dma((2,)),
             dma((1,)), dma((NCH + EX,)), dma((1,)), dma(((NCH + EX + 1) // 2,)), dma((1,)), dma((NQ,)), dma((1,)), dma((NQ,)),
             dma((5,)), dma((5,)),

time: 52.5 us -> 51.8 us (0.987)
  Pallas kernels: 49.6 us -> 48.9 us
    pallas_call x1, Pallas kernels: 49.6 us -> 48.9 us  [local(): pl.pallas_call(kernel, out_shape=(pltpu.VMEM((SAMPLES, SHARD), BF16), plt...]
where the time goes in v8:
time: 51.8 us; the launch traced here: 51.7 us
  Pallas kernels  48.9 us (94%)
  local copies, waits for them, and re-layouts  1.46 us (3%)
  between operations  1.29 us (2%)
    pallas_call x1, Pallas kernels, local(): pl.pallas_call(kernel, out_shape=(pltpu.VMEM((SAMPLES, SHARD), BF16), plt...  48.9 us
    unnamed x2, local copies, waits for them, and re-layouts  1.46 us

profile of v8, /device:TPU:32, one launch (start us, length us, event | category | flops | bytes accessed | tf_op | source)
XLA Modules:
  0.0 51.7 jit_solution(7253374731408572085)
XLA Ops:
  1.3 48.9 %shard_map.122 = (bf16[16,1280]{1,0:T(8,128)(2,1)S(1)}, bf16[256,1280]{1,0:T(8,128)(2,1)S(1)}) custom-call(s32[16]{0:T(128)} %so_hbm.1, s32[16]{0:T(128)} %sl_hbm.1, s32[1]{0:T(128)S(6)} %copy.17.pfl_hbm, bf16[16,1024]{1,0:T(8,128)(2,1)} %dq_hbm.1, bf16[16,2,128]{2,1,0:T(2,128)(2,1)} %nkv_hbm.1, bf16[256,2,128]{2,1,0:T(2,128)(2,1)} %pkv_hbm.1, ...), custom_call_target="tpu_custom_call" | custom-call | tf_op jit(solution)/shard_map/pallas_call | solution.py:705
  50.2 0.6 %copy.15 = bf16[16,1280]{1,0:T(8,128)(2,1)} copy(bf16[16,1280]{1,0:T(8,128)(2,1)S(1)} %get-tuple-element.2) | data formatting | bytes 81920
  50.8 0.8 %copy.16 = bf16[256,1280]{1,0:T(8,128)(2,1)} copy(bf16[256,1280]{1,0:T(8,128)(2,1)S(1)} %get-tuple-element.3) | data formatting | bytes 1310720

commit v9 on v8

--- a/solution.py
+++ b/solution.py
@@ -654,10 +654,10 @@
     decode_own(0)
     quarter(5)
     decode_own(2)
+    on_mid(decode_across)
     on_mid(decode_to_edge)
+    quarter(6)
     decode_own(3)
-    on_mid(decode_across)
-    quarter(6)
     on_mid(sent_early)
     quarter(7)
     on_edge(edge_finals)

time: 51.8 us -> 51.8 us (level)
  no operation moved by 1% of the time
where the time goes in v9:
time: 51.8 us; the launch traced here: 51.7 us
  Pallas kernels  48.9 us (94%)
  local copies, waits for them, and re-layouts  1.46 us (3%)
  between operations  1.29 us (2%)
    pallas_call x1, Pallas kernels, local(): pl.pallas_call(kernel, out_shape=(pltpu.VMEM((SAMPLES, SHARD), BF16), plt...  48.9 us
    unnamed x2, local copies, waits for them, and re-layouts  1.46 us

profile of v9, /device:TPU:32, one launch (start us, length us, event | category | flops | bytes accessed | tf_op | source)
XLA Modules:
  0.0 51.7 jit_solution(4671881287113454505)
XLA Ops:
  1.3 48.9 %shard_map.122 = (bf16[16,1280]{1,0:T(8,128)(2,1)S(1)}, bf16[256,1280]{1,0:T(8,128)(2,1)S(1)}) custom-call(s32[16]{0:T(128)} %so_hbm.1, s32[16]{0:T(128)} %sl_hbm.1, s32[1]{0:T(128)S(6)} %copy.17.pfl_hbm, bf16[16,1024]{1,0:T(8,128)(2,1)} %dq_hbm.1, bf16[16,2,128]{2,1,0:T(2,128)(2,1)} %nkv_hbm.1, bf16[256,2,128]{2,1,0:T(2,128)(2,1)} %pkv_hbm.1, ...), custom_call_target="tpu_custom_call" | custom-call | tf_op jit(solution)/shard_map/pallas_call | solution.py:705
  50.2 0.6 %copy.15 = bf16[16,1280]{1,0:T(8,128)(2,1)} copy(bf16[16,1280]{1,0:T(8,128)(2,1)S(1)} %get-tuple-element.2) | data formatting | bytes 81920
  50.8 0.8 %copy.16 = bf16[256,1280]{1,0:T(8,128)(2,1)} copy(bf16[256,1280]{1,0:T(8,128)(2,1)S(1)} %get-tuple-element.3) | data formatting | bytes 1310720
